TPU v7x, 32 devices: a whole 2x2x4 slice. The times are simulated.
32 devices in a mesh: grp: 2 (over y), sec: 4 (over z), op: 2 (over x), rep: 2 (over core).
Axes of the slice: x: 2, y: 2, z: 4, core: 2. Of those that a mesh axis runs over, the one named last changes fastest.
Arguments:
- psi: bfloat16 [32, 256, 256], P(('grp', 'sec'), 'rep'), parts along dimension 0, may hold values from -6 to 6
- left_env: bfloat16 [32, 16, 256, 256], P(('grp', 'op'), 'sec', 'rep'), parts along dimension 0, may hold values from -0.09375 to 0.09375
- right_env: bfloat16 [32, 256, 256], P(('grp', 'op')), parts along dimension 0, may hold values from -0.375 to 0.375
- pairing: int32 [32, 16], P(('grp', 'op'), 'sec'), parts along dimension 0, may hold values from 0 to 15, as said below
- block_rows: int32 [32], P(('grp', 'sec')), parts along dimension 0, may hold values from 64 to 256, as said below
- block_cols: int32 [32], P(('grp', 'sec')), parts along dimension 0, may hold values from 64 to 256, as said below
- energy: float32 [32, 256], P(('grp', 'sec'), 'rep'), parts along dimension 0, may hold values from 1 to 4
Outputs:
- sigma_first: bfloat16 [32, 256, 256], P(('grp', 'sec'), 'rep'), parts along dimension 0
- sigma_second: bfloat16 [32, 256, 256], P(('grp', 'sec'), 'rep'), parts along dimension 0
There are 2 independent parts, one for each index of `grp`. A program takes and returns all parts, laid end to end along the dimension named above; each array names one. Nothing has to cross between parts.
Inputs may be any that keep to these rules, and one draw needn't show every extreme that they name: `pairing`: the 8 x 4 entries of one op index and one sec index name sectors of any one sec index at most 9 times, and all of them that name sectors of one sec index name the same sector; in every op index some sec index is named exactly 9 times from every sec index. `block_rows`: some sector has exactly 256 live rows. `block_cols`: some sector has exactly 256 live columns.
All inputs are finite; a program needn't handle non-finite values.
Results may differ from a plain program's by a relative error of at most 0.0085.
Values may be sent and summed in bfloat16 or wider, within the bound.
No kernel may reach another device: no remote copies, remote signals or barrier semaphores. Data moves between devices by JAX's collectives and lax.ppermute only.
A program may use at most 64 MiB of HBM per device.

v0:
```python
import functools

import jax
import jax.numpy as jnp
from jax import lax
from jax.experimental import pallas as pl
from jax.experimental.pallas import tpu as pltpu
from jax.sharding import PartitionSpec as P

EPSILON = 1e-06
HEAD = 8
PARTS = 3
MORE_ROWS = 16
LANES = 128
VMEM_BYTES = 24 * 1024 * 1024
F32 = jnp.float32
BF16 = jnp.bfloat16


def whole(space):
    return pl.BlockSpec(memory_space=space)


def live(limit_ref, s, first_row, shape):
    sec_dev = limit_ref.shape[0] // 2
    repeat = shape[1] // LANES
    rows = jnp.concatenate([limit_ref[s:s + 1, :]] * repeat, axis=1)
    cols = jnp.concatenate([limit_ref[sec_dev + s:sec_dev + s + 1, :]] * repeat, axis=1)
    row_ids = first_row + lax.broadcasted_iota(jnp.int32, shape, 0)
    col_ids = lax.broadcasted_iota(jnp.int32, shape, 1)
    return (row_ids < rows) & (col_ids < cols)


def energy_columns(level):
    missing = -level.shape[0] % 8
    if missing:
        level = jnp.concatenate([level, jnp.zeros((missing, level.shape[1]), F32)], axis=0)
    return level.T


def spread(array, width):
    return jnp.concatenate([array] * (width // LANES), axis=1)


def quotient(value, count):
    return value >> (count.bit_length() - 1) if count & (count - 1) == 0 else lax.div(value, count)


def remainder(value, count):
    return value & (count - 1) if count & (count - 1) == 0 else lax.rem(value, count)


def fold(array):
    rows, width = array.shape
    return jnp.sum(array.reshape(rows // 8, 8, width), axis=0)


def total(array):
    return jnp.sum(jnp.sum(array, axis=0, keepdims=True), axis=1, keepdims=True)


def header(slot, scalars, shape=(HEAD, LANES)):
    row_ids = lax.broadcasted_iota(jnp.int32, shape, 0)
    head = jnp.where(row_ids == 0, slot.astype(F32), 0.0)
    row = 1
    for scalar in scalars:
        rest = jnp.broadcast_to(scalar, shape)
        for _ in range(PARTS):
            piece = rest.astype(BF16).astype(F32)
            head = jnp.where(row_ids == row, piece, head)
            rest = rest - piece
            row += 1
    return head.astype(BF16)


def head_scalar(head_sum, index):
    first = 1 + PARTS * index
    return jnp.sum(head_sum[first:first + PARTS], axis=0, keepdims=True)


def most_pairs(pairs, sec_count):
    return pairs // sec_count + 1


def load_kernel(
    psi_hbm, left_hbm, right_hbm, pairing_hbm, rows_hbm, cols_hbm, energy_hbm,
    start_ref, left_ref, right_ref, list_ref, limit_ref, energy_ref, scalar_ref,
    psi_ref, level_ref, rows_ref, cols_ref, pairing_ref, entry_ref, count_ref, sems,
):
    sec_dev, half, width = psi_ref.shape
    terms = left_ref.shape[0]
    sec_count = list_ref.shape[0]
    cap = most_pairs(terms * sec_dev, sec_count)
    pairs = [
        (rows_hbm, rows_ref), (cols_hbm, cols_ref), (energy_hbm, level_ref),
        (pairing_hbm, pairing_ref), (psi_hbm, psi_ref),
    ]
    for t in range(left_ref.shape[0]):
        pairs.append((left_hbm.at[t], left_ref.at[t]))
        pairs.append((right_hbm.at[t], right_ref.at[t]))
    copies = [
        pltpu.make_async_copy(source, target, sems.at[i])
        for i, (source, target) in enumerate(pairs)
    ]
    for copy in copies:
        copy.start()
    for owner in range(sec_count):
        count_ref[owner] = 0
        entry_ref[owner, cap] = 0
        for i in range(cap):
            entry_ref[owner, i] = terms * sec_dev
    for copy in copies[:3]:
        copy.wait()
    for s in range(sec_dev):
        limit_ref[s:s + 1, :] = jnp.full((1, LANES), rows_ref[s], jnp.int32)
        limit_ref[sec_dev + s:sec_dev + s + 1, :] = jnp.full((1, LANES), cols_ref[s], jnp.int32)
    columns = energy_columns(level_ref[...])
    for s in range(sec_dev):
        energy_ref[s] = jnp.broadcast_to(columns[:, s:s + 1], (half, LANES))
    copies[3].wait()
    for t in range(terms):
        for s in range(sec_dev):
            target = pairing_ref[s, t]
            owner = quotient(target, sec_dev)
            count = count_ref[owner]
            entry_ref[owner, count] = t * sec_dev + s
            entry_ref[owner, cap] = remainder(target, sec_dev)
            count_ref[owner] = count + 1
    entries = pltpu.make_async_copy(entry_ref, list_ref, sems.at[len(copies)])
    entries.start()
    copies[4].wait()
    first_row = lax.axis_index("rep") * half
    norm = jnp.zeros((8, width), F32)
    level = jnp.zeros((8, width), F32)
    for s in range(sec_dev):
        vector = jnp.where(
            live(limit_ref, s, first_row, (half, width)), psi_ref[s].astype(F32), 0.0
        )
        start_ref[s] = vector.astype(BF16)
        square = vector * vector
        norm += fold(square)
        level += fold(square * spread(energy_ref[s], width))
    scalar_ref[0:8, :] = norm
    scalar_ref[8:16, :] = level
    for copy in copies[5:]:
        copy.wait()
    entries.wait()


def product_kernel(is_first, split, paired, rep_count, sec_count, *refs):
    refs = list(refs)
    take = lambda count: [refs.pop(0) for _ in range(count)]
    list_ref, left_ref, right_ref = take(3)
    if is_first:
        start_ref, limit_ref, scalar_ref = take(3)
        psi_refs = take(rep_count - 1)
        level_refs = take(rep_count - 1)
    else:
        vector_refs = take(rep_count)
    out_refs = take(sec_count if split else 1)
    inner_ref, entry_ref, sem = refs
    terms, sec_dev, half, width = left_ref.shape
    pairs = terms * sec_dev
    cap = most_pairs(pairs, sec_count)
    rep = lax.axis_index("rep")
    sec = lax.axis_index("sec")
    fetch = pltpu.make_async_copy(list_ref, entry_ref, sem)
    fetch.start()
    inner_ref[pairs] = jnp.zeros((half, width), BF16)

    def first_row(step):
        return remainder(rep + step, rep_count) * half

    if is_first:
        folded = [scalar_ref[0:8, :], scalar_ref[8:16, :]]
        columns = [energy_columns(ref[...]) for ref in level_refs]
    for s in range(sec_dev):
        if is_first:
            blocks = [start_ref[s]]
            for step in range(1, rep_count):
                psi = psi_refs[step - 1][s]
                mask = live(limit_ref, s, first_row(step), (half, width))
                blocks.append(jnp.where(mask, psi.astype(F32), 0.0).astype(BF16))
        else:
            blocks = [ref[s * half:(s + 1) * half] for ref in vector_refs]
        vector = jnp.concatenate(blocks, axis=0)
        for turn in range(1, rep_count):
            turned = blocks[rep_count - turn:] + blocks[:rep_count - turn]
            vector = jnp.where(rep == turn, jnp.concatenate(turned, axis=0), vector)
        inner = jnp.dot(
            left_ref[:, s].reshape(terms * half, width), vector, preferred_element_type=F32
        ).astype(BF16)
        for t in range(terms):
            inner_ref[t * sec_dev + s] = inner[t * half:(t + 1) * half]
        if is_first:
            for step in range(1, rep_count):
                block = blocks[step].astype(F32)
                square = block * block
                energy = jnp.broadcast_to(columns[step - 1][:, s:s + 1], (half, width))
                folded = [folded[0] + fold(square), folded[1] + fold(square * energy)]
    if is_first:
        scalars = [total(array) for array in folded]
    else:
        head = sum(ref[sec_dev * half:].astype(F32) for ref in vector_refs)
        scalars = [head_scalar(head, i)[:, :LANES] for i in range(2)]
    fetch.wait()
    for d in range(sec_count):
        if not split:
            owner = d
        elif paired:
            owner = sec ^ d
        else:
            owner = remainder(sec + d, sec_count)
        packet = jnp.zeros((half, width), F32)
        for i in range(cap):
            pair = entry_ref[owner, i]
            term = jnp.minimum(quotient(pair, sec_dev), terms - 1)
            packet += jnp.dot(inner_ref[pair], right_ref[term], preferred_element_type=F32)
        out = out_refs[d] if split else out_refs[0].at[d]
        for column in range(width // LANES):
            out[column * half:(column + 1) * half, :] = packet[
                :, column * LANES:(column + 1) * LANES
            ].astype(BF16)
        out[width // LANES * half:, :] = header(entry_ref[owner, cap], scalars)


def sigma_packets(is_first, split, paired, rep_count, lists, left_env, right_env, more):
    terms, sec_dev, half, width = left_env.shape
    sec_count = lax.axis_size("sec")
    packet = (width // LANES * half + HEAD, LANES)
    if split:
        outs = [jax.ShapeDtypeStruct(packet, BF16)] * sec_count
    else:
        outs = [jax.ShapeDtypeStruct((sec_count,) + packet, BF16)]
    pair_flops = 2 * half * width * width * 2
    operands = [lists, left_env, right_env, *more]
    return pl.pallas_call(
        functools.partial(product_kernel, is_first, split, paired, rep_count, sec_count),
        out_shape=outs,
        in_specs=[whole(pltpu.VMEM)] * len(operands),
        out_specs=[whole(pltpu.VMEM)] * len(outs),
        scratch_shapes=[
            pltpu.VMEM((terms * sec_dev + 1, half, width), BF16),
            pltpu.SMEM(lists.shape, jnp.int32),
            pltpu.SemaphoreType.DMA,
        ],
        compiler_params=pltpu.CompilerParams(vmem_limit_bytes=VMEM_BYTES),
        cost_estimate=pl.CostEstimate(
            flops=terms * sec_dev * pair_flops,
            bytes_accessed=2 * (left_env.size + right_env.size),
            transcendentals=0,
        ),
        name="products_first" if is_first else "products_second",
    )(*operands)


def exchange(packets, split, paired, order, own_at):
    sec_count = lax.axis_size("sec")
    op_count = lax.axis_size("op")
    op_turns = [
        [(i, (i + step) % op_count) for i in range(op_count)] for step in range(1, op_count)
    ]
    over_op = lambda packet: [lax.ppermute(packet, "op", turn) for turn in op_turns]
    if not split:
        arrived = lax.all_to_all(packets[0], "sec", split_axis=0, concat_axis=0, tiled=True)
        return [arrived] + over_op(arrived), []
    arrived = {0: packets[0]}
    crossed = {}
    for position, step in enumerate(order):
        if position == own_at:
            crossed[0] = over_op(packets[0])
        reach = (lambda i: i ^ step) if paired else (lambda i: (i + step) % sec_count)
        turn = [(i, reach(i)) for i in range(sec_count)]
        arrived[step] = lax.ppermute(packets[step], "sec", turn)
    if own_at >= len(order):
        crossed[0] = over_op(packets[0])
    for step in order:
        crossed[step] = over_op(arrived[step])
    steps = [0, *order]
    gathered = [arrived[step] for step in steps] + sum([crossed[step] for step in steps], [])
    return gathered[:-1], gathered[-1:]


def add_packets(packet_refs, split, half, base_ref):
    sec_dev, _, width = base_ref.shape
    own = lax.axis_size("sec") if split else 1
    body_rows = width // LANES * half
    if split:
        heads = [ref[body_rows:].astype(F32) for ref in packet_refs]
        for column in range(width // LANES):
            lanes = slice(column * LANES, (column + 1) * LANES)
            for s in range(sec_dev):
                part = base_ref[s, :, lanes]
                for ref, head in zip(packet_refs, heads):
                    body = ref[column * half:(column + 1) * half].astype(F32)
                    part += jnp.where(head[0:1] == s, body, 0.0)
                base_ref[s, :, lanes] = part
        return sum(heads[1:own], heads[0])

    head_sum = jnp.zeros((HEAD, LANES), F32)
    for index, ref in enumerate(packet_refs):
        def add_one(p, carry):
            head = ref[p, body_rows:, :].astype(F32)
            for column in range(width // LANES):
                body = ref[p, column * half:(column + 1) * half, :].astype(F32)
                lanes = slice(column * LANES, (column + 1) * LANES)
                for s in range(sec_dev):
                    base_ref[s, :, lanes] += jnp.where(head[0:1] == s, body, 0.0)
            return carry + head
        result = lax.fori_loop(0, ref.shape[0], add_one, jnp.zeros((HEAD, LANES), F32))
        if index < own:
            head_sum = head_sum + result
    return head_sum


def late_sum(packet_refs, s, half, width):
    body_rows = width // LANES * half
    value = jnp.zeros((half, width), F32)
    for ref in packet_refs:
        body = jnp.concatenate(
            [ref[c * half:(c + 1) * half].astype(F32) for c in range(width // LANES)], axis=1
        )
        slot = spread(ref[body_rows:].astype(F32)[0:1], width)
        value += jnp.where(slot == s, body, 0.0)
    return value


def first_early_kernel(split, count, *refs):
    packet_refs = refs[:count]
    start_ref, energy_ref, base_ref, scalar_ref = refs[count:]
    sec_dev, half, width = start_ref.shape
    for s in range(sec_dev):
        base_ref[s] = spread(energy_ref[s], width) * start_ref[s].astype(F32)
    head_sum = add_packets(packet_refs, split, half, base_ref)
    norm = head_scalar(head_sum, 0)
    scalar_ref[0:1] = norm
    scalar_ref[1:2] = head_scalar(head_sum, 1) / norm


def first_kernel(count, *refs):
    packet_refs = refs[:count]
    limit_ref, start_ref, base_ref, scalar_ref, first_ref, one_ref, vec_ref = refs[count:]
    sec_dev, half, width = start_ref.shape
    shift = spread(scalar_ref[1:2], width)
    first_row = lax.axis_index("rep") * half
    cross = jnp.zeros((8, width), F32)
    square = jnp.zeros((8, width), F32)
    for s in range(sec_dev):
        mask = live(limit_ref, s, first_row, (half, width))
        start = start_ref[s].astype(F32)
        one = jnp.where(mask, base_ref[s] + late_sum(packet_refs, s, half, width), 0.0)
        one_ref[s] = one
        first_ref[s] = one.astype(BF16)
        vector = one - shift * start
        vec_ref[s * half:(s + 1) * half] = vector.astype(BF16)
        cross += fold(start * vector)
        square += fold(vector * vector)
    scalars = (total(cross), total(square))
    vec_ref[sec_dev * half:] = header(jnp.int32(0), scalars, (MORE_ROWS, width))


def second_early_kernel(split, count, entries, *refs):
    packet_refs = refs[:count]
    vec_ref, energy_ref, one_ref, scalar_ref, base_ref, scale_ref = refs[count:]
    sec_dev, half, width = one_ref.shape
    for s in range(sec_dev):
        vector = vec_ref[s * half:(s + 1) * half].astype(F32)
        base_ref[s] = spread(energy_ref[s], width) * vector
    head_sum = add_packets(packet_refs, split, half, base_ref)
    cross = head_scalar(head_sum, 0)
    square = head_scalar(head_sum, 1)
    excess = cross / scalar_ref[0:1]
    resid_sq = jnp.maximum(square - excess * cross, 0.0)
    scale = lax.rsqrt(resid_sq / entries + EPSILON)
    scale_ref[...] = jnp.broadcast_to(scale, scale_ref.shape)
    for s in range(sec_dev):
        base_ref[s] = base_ref[s] - spread(excess, width) * one_ref[s]


def second_kernel(count, *refs):
    packet_refs = refs[:count]
    limit_ref, base_ref, scale_ref, second_ref = refs[count:]
    sec_dev, half, width = base_ref.shape
    scale = spread(scale_ref[0:1], width)
    first_row = lax.axis_index("rep") * half
    for s in range(sec_dev):
        mask = live(limit_ref, s, first_row, (half, width))
        value = scale * (base_ref[s] + late_sum(packet_refs, s, half, width))
        second_ref[s] = jnp.where(mask, value, 0.0).astype(BF16)


def call(kernel, name, outs, *operands):
    return pl.pallas_call(
        kernel,
        out_shape=outs,
        in_specs=[whole(pltpu.VMEM)] * len(operands),
        out_specs=[whole(pltpu.VMEM)] * len(outs),
        compiler_params=pltpu.CompilerParams(vmem_limit_bytes=VMEM_BYTES),
        name=name,
    )(*operands)


def body(psi, left_env, right_env, pairing, block_rows, block_cols, energy):
    sec_count = lax.axis_size("sec")
    op_count = lax.axis_size("op")
    rep_count = lax.axis_size("rep")
    terms, sec_dev, half, width = left_env.shape
    entries = sec_count * sec_dev * rep_count * half * width
    split = sec_count * op_count <= 8
    can_pair = sec_count & (sec_count - 1) == 0
    steps = list(range(1, sec_count))
    first_plan = (False, steps, sec_count - 1)
    second_plan = (can_pair, steps[1:2] + steps[:1] + steps[2:], sec_count - 1)
    params = pltpu.CompilerParams(vmem_limit_bytes=VMEM_BYTES)
    vec_shape = (sec_dev, half, width)
    vec_bf16 = jax.ShapeDtypeStruct(vec_shape, BF16)

    def from_others(array):
        arrays = []
        for step in range(1, rep_count):
            turn = [((i + step) % rep_count, i) for i in range(rep_count)]
            arrays.append(lax.ppermute(array, "rep", turn))
        return arrays

    psi_others = from_others(psi)
    level_others = from_others(energy)
    start, left_env, right_env, lists, limits, levels, scalars = pl.pallas_call(
        load_kernel,
        out_shape=[
            vec_bf16,
            jax.ShapeDtypeStruct(left_env.shape, BF16),
            jax.ShapeDtypeStruct(right_env.shape, BF16),
            jax.ShapeDtypeStruct((sec_count, LANES), jnp.int32),
            jax.ShapeDtypeStruct((2 * sec_dev, LANES), jnp.int32),
            jax.ShapeDtypeStruct((sec_dev, half, LANES), F32),
            jax.ShapeDtypeStruct((16, width), F32),
        ],
        in_specs=[whole(pltpu.HBM)] * 7,
        out_specs=[whole(pltpu.VMEM)] * 7,
        scratch_shapes=[
            pltpu.VMEM(vec_shape, BF16),
            pltpu.VMEM((sec_dev, half), F32),
            pltpu.SMEM((sec_dev,), jnp.int32),
            pltpu.SMEM((sec_dev,), jnp.int32),
            pltpu.SMEM((sec_dev, terms), jnp.int32),
            pltpu.SMEM((sec_count, LANES), jnp.int32),
            pltpu.SMEM((sec_count,), jnp.int32),
            pltpu.SemaphoreType.DMA((6 + 2 * terms,)),
        ],
        compiler_params=params,
        name="load",
    )(*(
        pltpu.with_memory_space_constraint(array, pltpu.HBM)
        for array in (psi, left_env, right_env, pairing.T, block_rows, block_cols, energy)
    ))

    block_f32 = jax.ShapeDtypeStruct(vec_shape, F32)
    row_f32 = jax.ShapeDtypeStruct((8, LANES), F32)

    packets = sigma_packets(
        True, split, first_plan[0], rep_count, lists, left_env, right_env,
        [start, limits, scalars, *psi_others, *level_others],
    )
    early, late = exchange(packets, split, *first_plan)
    base, scalars = call(
        functools.partial(first_early_kernel, split, len(early)), "combine_first_early",
        [block_f32, row_f32], *early, start, levels,
    )
    first_out, sigma_one, vector = call(
        functools.partial(first_kernel, len(late)), "combine_first",
        [
            pltpu.VMEM(vec_shape, BF16),
            block_f32,
            jax.ShapeDtypeStruct((sec_dev * half + MORE_ROWS, width), BF16),
        ],
        *late, limits, start, base, scalars,
    )

    packets = sigma_packets(
        False, split, second_plan[0], rep_count, lists, left_env, right_env,
        [vector, *from_others(vector)],
    )
    early, late = exchange(packets, split, *second_plan)
    base, scale = call(
        functools.partial(second_early_kernel, split, len(early), entries),
        "combine_second_early", [block_f32, row_f32], *early, vector, levels, sigma_one, scalars,
    )
    (second_out,) = call(
        functools.partial(second_kernel, len(late)), "combine_second", [vec_bf16],
        *late, limits, base, scale,
    )
    return (first_out, second_out)


def solution(mesh):
    return jax.shard_map(
        body,
        mesh=mesh,
        in_specs=(
            P(("grp", "sec"), "rep", None),
            P(("grp", "op"), "sec", "rep", None),
            P(("grp", "op"), None, None),
            P(("grp", "op"), "sec"),
            P(("grp", "sec")),
            P(("grp", "sec")),
            P(("grp", "sec"), "rep"),
        ),
        out_specs=(P(("grp", "sec"), "rep", None), P(("grp", "sec"), "rep", None)),
        check_vma=False,
    )
```

profile of v0, /device:TPU:0, one launch (start us, length us, event | category | flops | bytes accessed | tf_op | source)
XLA Modules:
  0.0 39.7 jit_solution(16174596600074078605)
XLA Ops:
  0.6 0.5 %collective-permute-start = (bf16[4,128,256]{2,1,0:T(8,128)(2,1)}, bf16[4,128,256]{2,1,0:T(8,128)(2,1)S(1)}, u32[]{:S(2)}, u32[]{:S(2)}) collective-permute-start(bf16[4,128,256]{2,1,0:T(8,128)(2,1)} %psi_hbm.1), channel_id=1, source_target_pairs={{1,0},{0,1},{3,2},{2,3},{5,4},{4,5},{7,6},{6,7},{9,8},{8,9},{11,10... | collective-permute-start | bytes 786440 | tf_op jit(solution)/shard_map/ppermute | solution.py:422
  1.1 0.1 collective-permute-start.1
  1.2 2.1 %load.1 = (bf16[4,128,256]{2,1,0:T(8,128)(2,1)S(1)}, bf16[8,4,128,256]{3,2,1,0:T(8,128)(2,1)S(1)}, bf16[8,256,256]{2,1,0:T(8,128)(2,1)S(1)}, s32[4,128]{1,0:T(4,...) custom-call(bf16[4,128,256]{2,1,0:T(8,128)(2,1)} %psi_hbm.1, ...), custom_call_target="tpu_custom_call" | custom-call | tf_op jit(solution)/shard_map/load/pallas_call | solution.py:427
  3.3 0.0 collective-permute-done.1.refs_7_
  3.4 0.0 collective-permute-done.refs_6_
  3.4 1.6 %products_first.1 = (bf16[264,128]{1,0:T(8,128)(2,1)S(1)}, bf16[264,128]{1,0:T(8,128)(2,1)S(1)}, bf16[264,128]{1,0:T(8,128)(2,1)S(1)}, bf16[264,128]{1,0:T(8,128)(2,1)S(1)}) custom-call(s32[4,128]{1,0:T(4,128)S(1)} %get-tuple-element.24.refs_0_, bf16[8,4,128,256]{3,2,1,0:T(8,128)(2,1)S(1)} %get-tuple-element.25.refs_1_, ...), custom_call_target="tpu_custom_call" | custom-call | flops 1073741824 | bytes 3145728 | tf_op jit(solution)/shard_map/products_first/pallas_call | solution.py:237
  4.9 3.1 %collective-permute-start.4 = (bf16[264,128]{1,0:T(8,128)(2,1)S(1)}, bf16[264,128]{1,0:T(8,128)(2,1)S(1)}, u32[]{:S(2)}, u32[]{:S(2)}) collective-permute-start(bf16[264,128]{1,0:T(8,128)(2,1)S(1)} %get-tuple-element.32), channel_id=1, source_target_pairs={{0,4},{4,8},{8,12},{12,0},{1,5},{5,9},{9,13},{13,1},{2,6},{6,10},{... | collective-permute-start | bytes 202760 | tf_op jit(solution)/shard_map/ppermute | solution.py:274
  8.0 2.6 %collective-permute-start.5 = (bf16[264,128]{1,0:T(8,128)(2,1)S(1)}, bf16[264,128]{1,0:T(8,128)(2,1)S(1)}, u32[]{:S(2)}, u32[]{:S(2)}) collective-permute-start(bf16[264,128]{1,0:T(8,128)(2,1)S(1)} %get-tuple-element.33), channel_id=1, source_target_pairs={{0,8},{4,12},{8,0},{12,4},{1,9},{5,13},{9,1},{13,5},{2,10},{6,14},... | collective-permute-start | bytes 202760 | tf_op jit(solution)/shard_map/ppermute | solution.py:274
  10.6 1.3 %collective-permute-start.2 = (bf16[264,128]{1,0:T(8,128)(2,1)S(1)}, bf16[264,128]{1,0:T(8,128)(2,1)S(1)}, u32[]{:S(2)}, u32[]{:S(2)}) collective-permute-start(bf16[264,128]{1,0:T(8,128)(2,1)S(1)} %get-tuple-element.30), channel_id=1, source_target_pairs={{0,12},{4,0},{8,4},{12,8},{1,13},{5,1},{9,5},{13,9},{2,14},{6,2},{... | collective-permute-start | bytes 202760 | tf_op jit(solution)/shard_map/ppermute | solution.py:274
  11.9 1.5 %collective-permute-start.6 = (bf16[264,128]{1,0:T(8,128)(2,1)S(1)}, bf16[264,128]{1,0:T(8,128)(2,1)S(1)}, u32[]{:S(2)}, u32[]{:S(2)}) collective-permute-start(bf16[264,128]{1,0:T(8,128)(2,1)S(1)} %get-tuple-element.31.refs_0_), channel_id=1, source_target_pairs={{0,2},{2,0},{1,3},{3,1},{4,6},{6,4},{5,7},{7,5},{8,10},{10,8},{9,1... | collective-permute-start | bytes 202760 | tf_op jit(solution)/shard_map/ppermute | solution.py:263
  13.4 0.0 collective-permute-done.4.refs_1_
  13.4 0.9 %collective-permute-start.7 = (bf16[264,128]{1,0:T(8,128)(2,1)S(1)}, bf16[264,128]{1,0:T(8,128)(2,1)S(1)}, u32[]{:S(2)}, u32[]{:S(2)}) collective-permute-start(bf16[264,128]{1,0:T(8,128)(2,1)S(1)} %collective-permute-done.4.refs_1_), channel_id=1, source_target_pairs={{0,2},{2,0},{1,3},{3,1},{4,6},{6,4},{5,7},{7,5},{8,10},{10,8},{9,1... | collective-permute-start | bytes 202760 | tf_op jit(solution)/shard_map/ppermute | solution.py:263
  14.3 1.1 %collective-permute-done.5.refs_2_ = bf16[264,128]{1,0:T(8,128)(2,1)S(1)} collective-permute-done((bf16[264,128]{1,0:T(8,128)(2,1)S(1)}, bf16[264,128]{1,0:T(8,128)(2,1)S(1)}, u32[]{:S(2)}, u32[]{:S(2)}) %collective-permute-start.5) | collective-permute-done | bytes 67616 | tf_op jit(solution)/shard_map/ppermute | solution.py:274
  15.4 1.5 %collective-permute-start.8 = (bf16[264,128]{1,0:T(8,128)(2,1)S(1)}, bf16[264,128]{1,0:T(8,128)(2,1)S(1)}, u32[]{:S(2)}, u32[]{:S(2)}) collective-permute-start(bf16[264,128]{1,0:T(8,128)(2,1)S(1)} %collective-permute-done.5.refs_2_), channel_id=1, source_target_pairs={{0,2},{2,0},{1,3},{3,1},{4,6},{6,4},{5,7},{7,5},{8,10},{10,8},{9,1... | collective-permute-start | bytes 202760 | tf_op jit(solution)/shard_map/ppermute | solution.py:263
  16.9 0.0 collective-permute-done.2.refs_3_
  16.9 0.5 %collective-permute-start.3 = (bf16[264,128]{1,0:T(8,128)(2,1)S(1)}, bf16[264,128]{1,0:T(8,128)(2,1)S(1)}, u32[]{:S(2)}, u32[]{:S(2)}) collective-permute-start(bf16[264,128]{1,0:T(8,128)(2,1)S(1)} %collective-permute-done.2.refs_3_), channel_id=1, source_target_pairs={{0,2},{2,0},{1,3},{3,1},{4,6},{6,4},{5,7},{7,5},{8,10},{10,8},{9,1... | collective-permute-start | bytes 202760 | tf_op jit(solution)/shard_map/ppermute | solution.py:263
  17.4 0.0 collective-permute-done.6.refs_4_
  17.4 0.3 collective-permute-done.7.refs_5_
  17.7 2.5 %collective-permute-done.8.refs_6_ = bf16[264,128]{1,0:T(8,128)(2,1)S(1)} collective-permute-done((bf16[264,128]{1,0:T(8,128)(2,1)S(1)}, bf16[264,128]{1,0:T(8,128)(2,1)S(1)}, u32[]{:S(2)}, u32[]{:S(2)}) %collective-permute-start.8) | collective-permute-done | bytes 67616 | tf_op jit(solution)/shard_map/ppermute | solution.py:263
  20.3 0.4 %combine_first_early.1 = (f32[4,128,256]{2,1,0:T(8,128)S(1)}, f32[8,128]{1,0:T(8,128)S(1)}) custom-call(bf16[264,128]{1,0:T(8,128)(2,1)S(1)} %get-tuple-element.31.refs_0_, bf16[264,128]{1,0:T(8,128)(2,1)S(1)} %collective-permute-done.4.refs_1_, bf16[264,128]{1,0:T(8,128)(2,1)S(1)} %collective-permute-done.5.refs_2_, ...), custom_call_target="tpu_custom_call" | custom-call | tf_op jit(solution)/shard_map/combine_first_early/pallas_call | solution.py:393
  20.7 0.5 %collective-permute-done.3.refs_0_ = bf16[264,128]{1,0:T(8,128)(2,1)S(1)} collective-permute-done((bf16[264,128]{1,0:T(8,128)(2,1)S(1)}, bf16[264,128]{1,0:T(8,128)(2,1)S(1)}, u32[]{:S(2)}, u32[]{:S(2)}) %collective-permute-start.3) | collective-permute-done | bytes 67616 | tf_op jit(solution)/shard_map/ppermute | solution.py:263
  21.2 0.4 combine_first.1
  21.6 0.1 collective-permute-start.9
  21.6 1.5 %collective-permute-done.9.refs_4_ = bf16[528,256]{1,0:T(8,128)(2,1)S(1)} collective-permute-done((bf16[528,256]{1,0:T(8,128)(2,1)S(1)}, bf16[528,256]{1,0:T(8,128)(2,1)S(1)}, u32[]{:S(2)}, u32[]{:S(2)}) %collective-permute-start.9) | collective-permute-done | bytes 270368 | tf_op jit(solution)/shard_map/ppermute | solution.py:422
  23.2 1.5 %products_second.1 = (bf16[264,128]{1,0:T(8,128)(2,1)S(1)}, bf16[264,128]{1,0:T(8,128)(2,1)S(1)}, bf16[264,128]{1,0:T(8,128)(2,1)S(1)}, bf16[264,128]{1,0:T(8,128)(2,1)S(1)}) custom-call(s32[4,128]{1,0:T(4,128)S(1)} %get-tuple-element.24.refs_0_, bf16[8,4,128,256]{3,2,1,0:T(8,128)(2,1)S(1)} %get-tuple-element.25.refs_1_, ...), custom_call_target="tpu_custom_call" | custom-call | flops 1073741824 | bytes 3145728 | tf_op jit(solution)/shard_map/products_second/pallas_call | solution.py:237
  24.7 1.1 %collective-permute-start.12 = (bf16[264,128]{1,0:T(8,128)(2,1)S(1)}, bf16[264,128]{1,0:T(8,128)(2,1)S(1)}, u32[]{:S(2)}, u32[]{:S(2)}) collective-permute-start(bf16[264,128]{1,0:T(8,128)(2,1)S(1)} %get-tuple-element.41), channel_id=1, source_target_pairs={{0,8},{4,12},{8,0},{12,4},{1,9},{5,13},{9,1},{13,5},{2,10},{6,14},... | collective-permute-start | bytes 202760 | tf_op jit(solution)/shard_map/ppermute | solution.py:274
  25.8 2.7 %collective-permute-start.13 = (bf16[264,128]{1,0:T(8,128)(2,1)S(1)}, bf16[264,128]{1,0:T(8,128)(2,1)S(1)}, u32[]{:S(2)}, u32[]{:S(2)}) collective-permute-start(bf16[264,128]{1,0:T(8,128)(2,1)S(1)} %get-tuple-element.42), channel_id=1, source_target_pairs={{0,4},{4,0},{8,12},{12,8},{1,5},{5,1},{9,13},{13,9},{2,6},{6,2},{1... | collective-permute-start | bytes 202760 | tf_op jit(solution)/shard_map/ppermute | solution.py:274
  28.4 0.7 %collective-permute-start.10 = (bf16[264,128]{1,0:T(8,128)(2,1)S(1)}, bf16[264,128]{1,0:T(8,128)(2,1)S(1)}, u32[]{:S(2)}, u32[]{:S(2)}) collective-permute-start(bf16[264,128]{1,0:T(8,128)(2,1)S(1)} %get-tuple-element.39), channel_id=1, source_target_pairs={{0,12},{4,8},{8,4},{12,0},{1,13},{5,9},{9,5},{13,1},{2,14},{6,10},... | collective-permute-start | bytes 202760 | tf_op jit(solution)/shard_map/ppermute | solution.py:274
  29.2 1.1 %collective-permute-start.14 = (bf16[264,128]{1,0:T(8,128)(2,1)S(1)}, bf16[264,128]{1,0:T(8,128)(2,1)S(1)}, u32[]{:S(2)}, u32[]{:S(2)}) collective-permute-start(bf16[264,128]{1,0:T(8,128)(2,1)S(1)} %get-tuple-element.40.refs_0_), channel_id=1, source_target_pairs={{0,2},{2,0},{1,3},{3,1},{4,6},{6,4},{5,7},{7,5},{8,10},{10,8},{9,1... | collective-permute-start | bytes 202760 | tf_op jit(solution)/shard_map/ppermute | solution.py:263
  30.2 1.6 %collective-permute-done.12.refs_1_ = bf16[264,128]{1,0:T(8,128)(2,1)S(1)} collective-permute-done((bf16[264,128]{1,0:T(8,128)(2,1)S(1)}, bf16[264,128]{1,0:T(8,128)(2,1)S(1)}, u32[]{:S(2)}, u32[]{:S(2)}) %collective-permute-start.12) | collective-permute-done | bytes 67616 | tf_op jit(solution)/shard_map/ppermute | solution.py:274
  31.8 0.9 %collective-permute-start.15 = (bf16[264,128]{1,0:T(8,128)(2,1)S(1)}, bf16[264,128]{1,0:T(8,128)(2,1)S(1)}, u32[]{:S(2)}, u32[]{:S(2)}) collective-permute-start(bf16[264,128]{1,0:T(8,128)(2,1)S(1)} %collective-permute-done.12.refs_1_), channel_id=1, source_target_pairs={{0,2},{2,0},{1,3},{3,1},{4,6},{6,4},{5,7},{7,5},{8,10},{10,8},{9,1... | collective-permute-start | bytes 202760 | tf_op jit(solution)/shard_map/ppermute | solution.py:263
  32.7 0.0 collective-permute-done.13.refs_2_
  32.7 1.2 %collective-permute-start.16 = (bf16[264,128]{1,0:T(8,128)(2,1)S(1)}, bf16[264,128]{1,0:T(8,128)(2,1)S(1)}, u32[]{:S(2)}, u32[]{:S(2)}) collective-permute-start(bf16[264,128]{1,0:T(8,128)(2,1)S(1)} %collective-permute-done.13.refs_2_), channel_id=1, source_target_pairs={{0,2},{2,0},{1,3},{3,1},{4,6},{6,4},{5,7},{7,5},{8,10},{10,8},{9,1... | collective-permute-start | bytes 202760 | tf_op jit(solution)/shard_map/ppermute | solution.py:263
  33.9 0.7 %collective-permute-done.10.refs_3_ = bf16[264,128]{1,0:T(8,128)(2,1)S(1)} collective-permute-done((bf16[264,128]{1,0:T(8,128)(2,1)S(1)}, bf16[264,128]{1,0:T(8,128)(2,1)S(1)}, u32[]{:S(2)}, u32[]{:S(2)}) %collective-permute-start.10) | collective-permute-done | bytes 67616 | tf_op jit(solution)/shard_map/ppermute | solution.py:274
  34.5 0.8 %collective-permute-start.11 = (bf16[264,128]{1,0:T(8,128)(2,1)S(1)}, bf16[264,128]{1,0:T(8,128)(2,1)S(1)}, u32[]{:S(2)}, u32[]{:S(2)}) collective-permute-start(bf16[264,128]{1,0:T(8,128)(2,1)S(1)} %collective-permute-done.10.refs_3_), channel_id=1, source_target_pairs={{0,2},{2,0},{1,3},{3,1},{4,6},{6,4},{5,7},{7,5},{8,10},{10,8},{9,1... | collective-permute-start | bytes 202760 | tf_op jit(solution)/shard_map/ppermute | solution.py:263
  35.3 0.7 %copy.9 = bf16[4,128,256]{2,1,0:T(8,128)(2,1)} copy(bf16[4,128,256]{2,1,0:T(8,128)(2,1)S(1)} %get-tuple-element.46) | data formatting | bytes 524288
  36.0 0.0 collective-permute-done.14.refs_4_
  36.0 0.6 %collective-permute-done.15.refs_5_ = bf16[264,128]{1,0:T(8,128)(2,1)S(1)} collective-permute-done((bf16[264,128]{1,0:T(8,128)(2,1)S(1)}, bf16[264,128]{1,0:T(8,128)(2,1)S(1)}, u32[]{:S(2)}, u32[]{:S(2)}) %collective-permute-start.15) | collective-permute-done | bytes 67616 | tf_op jit(solution)/shard_map/ppermute | solution.py:263
  36.6 1.0 %collective-permute-done.16.refs_6_ = bf16[264,128]{1,0:T(8,128)(2,1)S(1)} collective-permute-done((bf16[264,128]{1,0:T(8,128)(2,1)S(1)}, bf16[264,128]{1,0:T(8,128)(2,1)S(1)}, u32[]{:S(2)}, u32[]{:S(2)}) %collective-permute-start.16) | collective-permute-done | bytes 67616 | tf_op jit(solution)/shard_map/ppermute | solution.py:263
  37.6 0.5 %combine_second_early.1 = (f32[4,128,256]{2,1,0:T(8,128)S(1)}, f32[8,128]{1,0:T(8,128)S(1)}) custom-call(bf16[264,128]{1,0:T(8,128)(2,1)S(1)} %get-tuple-element.40.refs_0_, bf16[264,128]{1,0:T(8,128)(2,1)S(1)} %collective-permute-done.12.refs_1_, bf16[264,128]{1,0:T(8,128)(2,1)S(1)} %collective-permute-done.13.refs_2_, ...), custom_call_target="tpu_custom_call" | custom-call | tf_op jit(solution)/shard_map/combine_second_early/pallas_call | solution.py:393
  38.1 0.7 %collective-permute-done.11.refs_0_ = bf16[264,128]{1,0:T(8,128)(2,1)S(1)} collective-permute-done((bf16[264,128]{1,0:T(8,128)(2,1)S(1)}, bf16[264,128]{1,0:T(8,128)(2,1)S(1)}, u32[]{:S(2)}, u32[]{:S(2)}) %collective-permute-start.11) | collective-permute-done | bytes 67616 | tf_op jit(solution)/shard_map/ppermute | solution.py:263
  38.8 0.8 %combine_second.1 = bf16[4,128,256]{2,1,0:T(8,128)(2,1)} custom-call(bf16[264,128]{1,0:T(8,128)(2,1)S(1)} %collective-permute-done.11.refs_0_, s32[8,128]{1,0:T(8,128)S(1)} %get-tuple-element.28.refs_4_.refs_1_, f32[4,128,256]{2,1,0:T(8,128)S(1)} %get-tuple-element.44.refs_2_, f32[8,128]{1,0:T(8,128)S(1)} %get-tuple-element.45.refs_3_), custom_call_target="tpu_custom_call" | custom-call | tf_op jit(solution)/shard_map/combine_second/pallas_call | solution.py:393
Async XLA Ops:
  0.6 2.7 %collective-permute-start = (bf16[4,128,256]{2,1,0:T(8,128)(2,1)}, bf16[4,128,256]{2,1,0:T(8,128)(2,1)S(1)}, u32[]{:S(2)}, u32[]{:S(2)}) collective-permute-start(bf16[4,128,256]{2,1,0:T(8,128)(2,1)} %psi_hbm.1), channel_id=1, source_target_pairs={{1,0},{0,1},{3,2},{2,3},{5,4},{4,5},{7,6},{6,7},{9,8},{8,9},{11,10... | collective-permute-start | bytes 786440 | tf_op jit(solution)/shard_map/ppermute | solution.py:422
  1.1 2.2 %collective-permute-start.1 = (f32[4,128]{1,0:T(4,128)}, f32[4,128]{1,0:T(4,128)S(1)}, u32[]{:S(2)}, u32[]{:S(2)}) collective-permute-start(f32[4,128]{1,0:T(4,128)} %energy_hbm.1), channel_id=1, source_target_pairs={{1,0},{0,1},{3,2},{2,3},{5,4},{4,5},{7,6},{6,7},{9,8},{8,9},{11,10... | collective-permute-start | bytes 6152 | tf_op jit(solution)/shard_map/ppermute | solution.py:422
  4.9 8.5 %collective-permute-start.4 = (bf16[264,128]{1,0:T(8,128)(2,1)S(1)}, bf16[264,128]{1,0:T(8,128)(2,1)S(1)}, u32[]{:S(2)}, u32[]{:S(2)}) collective-permute-start(bf16[264,128]{1,0:T(8,128)(2,1)S(1)} %get-tuple-element.32), channel_id=1, source_target_pairs={{0,4},{4,8},{8,12},{12,0},{1,5},{5,9},{9,13},{13,1},{2,6},{6,10},{... | collective-permute-start | bytes 202760 | tf_op jit(solution)/shard_map/ppermute | solution.py:274
  8.0 7.4 %collective-permute-start.5 = (bf16[264,128]{1,0:T(8,128)(2,1)S(1)}, bf16[264,128]{1,0:T(8,128)(2,1)S(1)}, u32[]{:S(2)}, u32[]{:S(2)}) collective-permute-start(bf16[264,128]{1,0:T(8,128)(2,1)S(1)} %get-tuple-element.33), channel_id=1, source_target_pairs={{0,8},{4,12},{8,0},{12,4},{1,9},{5,13},{9,1},{13,5},{2,10},{6,14},... | collective-permute-start | bytes 202760 | tf_op jit(solution)/shard_map/ppermute | solution.py:274
  10.6 6.3 %collective-permute-start.2 = (bf16[264,128]{1,0:T(8,128)(2,1)S(1)}, bf16[264,128]{1,0:T(8,128)(2,1)S(1)}, u32[]{:S(2)}, u32[]{:S(2)}) collective-permute-start(bf16[264,128]{1,0:T(8,128)(2,1)S(1)} %get-tuple-element.30), channel_id=1, source_target_pairs={{0,12},{4,0},{8,4},{12,8},{1,13},{5,1},{9,5},{13,9},{2,14},{6,2},{... | collective-permute-start | bytes 202760 | tf_op jit(solution)/shard_map/ppermute | solution.py:274
  11.9 5.5 %collective-permute-start.6 = (bf16[264,128]{1,0:T(8,128)(2,1)S(1)}, bf16[264,128]{1,0:T(8,128)(2,1)S(1)}, u32[]{:S(2)}, u32[]{:S(2)}) collective-permute-start(bf16[264,128]{1,0:T(8,128)(2,1)S(1)} %get-tuple-element.31.refs_0_), channel_id=1, source_target_pairs={{0,2},{2,0},{1,3},{3,1},{4,6},{6,4},{5,7},{7,5},{8,10},{10,8},{9,1... | collective-permute-start | bytes 202760 | tf_op jit(solution)/shard_map/ppermute | solution.py:263
  13.4 4.3 %collective-permute-start.7 = (bf16[264,128]{1,0:T(8,128)(2,1)S(1)}, bf16[264,128]{1,0:T(8,128)(2,1)S(1)}, u32[]{:S(2)}, u32[]{:S(2)}) collective-permute-start(bf16[264,128]{1,0:T(8,128)(2,1)S(1)} %collective-permute-done.4.refs_1_), channel_id=1, source_target_pairs={{0,2},{2,0},{1,3},{3,1},{4,6},{6,4},{5,7},{7,5},{8,10},{10,8},{9,1... | collective-permute-start | bytes 202760 | tf_op jit(solution)/shard_map/ppermute | solution.py:263
  15.4 4.9 %collective-permute-start.8 = (bf16[264,128]{1,0:T(8,128)(2,1)S(1)}, bf16[264,128]{1,0:T(8,128)(2,1)S(1)}, u32[]{:S(2)}, u32[]{:S(2)}) collective-permute-start(bf16[264,128]{1,0:T(8,128)(2,1)S(1)} %collective-permute-done.5.refs_2_), channel_id=1, source_target_pairs={{0,2},{2,0},{1,3},{3,1},{4,6},{6,4},{5,7},{7,5},{8,10},{10,8},{9,1... | collective-permute-start | bytes 202760 | tf_op jit(solution)/shard_map/ppermute | solution.py:263
  16.9 4.3 %collective-permute-start.3 = (bf16[264,128]{1,0:T(8,128)(2,1)S(1)}, bf16[264,128]{1,0:T(8,128)(2,1)S(1)}, u32[]{:S(2)}, u32[]{:S(2)}) collective-permute-start(bf16[264,128]{1,0:T(8,128)(2,1)S(1)} %collective-permute-done.2.refs_3_), channel_id=1, source_target_pairs={{0,2},{2,0},{1,3},{3,1},{4,6},{6,4},{5,7},{7,5},{8,10},{10,8},{9,1... | collective-permute-start | bytes 202760 | tf_op jit(solution)/shard_map/ppermute | solution.py:263
  21.6 1.6 %collective-permute-start.9 = (bf16[528,256]{1,0:T(8,128)(2,1)S(1)}, bf16[528,256]{1,0:T(8,128)(2,1)S(1)}, u32[]{:S(2)}, u32[]{:S(2)}) collective-permute-start(bf16[528,256]{1,0:T(8,128)(2,1)S(1)} %get-tuple-element.38.refs_3_.refs_7_), channel_id=1, source_target_pairs={{1,0},{0,1},{3,2},{2,3},{5,4},{4,5},{7,6},{6,7},{9,8},{8,9},{11,10... | collective-permute-start | bytes 811016 | tf_op jit(solution)/shard_map/ppermute | solution.py:422
  24.7 7.1 %collective-permute-start.12 = (bf16[264,128]{1,0:T(8,128)(2,1)S(1)}, bf16[264,128]{1,0:T(8,128)(2,1)S(1)}, u32[]{:S(2)}, u32[]{:S(2)}) collective-permute-start(bf16[264,128]{1,0:T(8,128)(2,1)S(1)} %get-tuple-element.41), channel_id=1, source_target_pairs={{0,8},{4,12},{8,0},{12,4},{1,9},{5,13},{9,1},{13,5},{2,10},{6,14},... | collective-permute-start | bytes 202760 | tf_op jit(solution)/shard_map/ppermute | solution.py:274
  25.8 7.0 %collective-permute-start.13 = (bf16[264,128]{1,0:T(8,128)(2,1)S(1)}, bf16[264,128]{1,0:T(8,128)(2,1)S(1)}, u32[]{:S(2)}, u32[]{:S(2)}) collective-permute-start(bf16[264,128]{1,0:T(8,128)(2,1)S(1)} %get-tuple-element.42), channel_id=1, source_target_pairs={{0,4},{4,0},{8,12},{12,8},{1,5},{5,1},{9,13},{13,9},{2,6},{6,2},{1... | collective-permute-start | bytes 202760 | tf_op jit(solution)/shard_map/ppermute | solution.py:274
  28.4 6.1 %collective-permute-start.10 = (bf16[264,128]{1,0:T(8,128)(2,1)S(1)}, bf16[264,128]{1,0:T(8,128)(2,1)S(1)}, u32[]{:S(2)}, u32[]{:S(2)}) collective-permute-start(bf16[264,128]{1,0:T(8,128)(2,1)S(1)} %get-tuple-element.39), channel_id=1, source_target_pairs={{0,12},{4,8},{8,4},{12,0},{1,13},{5,9},{9,5},{13,1},{2,14},{6,10},... | collective-permute-start | bytes 202760 | tf_op jit(solution)/shard_map/ppermute | solution.py:274
  29.2 6.8 %collective-permute-start.14 = (bf16[264,128]{1,0:T(8,128)(2,1)S(1)}, bf16[264,128]{1,0:T(8,128)(2,1)S(1)}, u32[]{:S(2)}, u32[]{:S(2)}) collective-permute-start(bf16[264,128]{1,0:T(8,128)(2,1)S(1)} %get-tuple-element.40.refs_0_), channel_id=1, source_target_pairs={{0,2},{2,0},{1,3},{3,1},{4,6},{6,4},{5,7},{7,5},{8,10},{10,8},{9,1... | collective-permute-start | bytes 202760 | tf_op jit(solution)/shard_map/ppermute | solution.py:263
  31.8 4.7 %collective-permute-start.15 = (bf16[264,128]{1,0:T(8,128)(2,1)S(1)}, bf16[264,128]{1,0:T(8,128)(2,1)S(1)}, u32[]{:S(2)}, u32[]{:S(2)}) collective-permute-start(bf16[264,128]{1,0:T(8,128)(2,1)S(1)} %collective-permute-done.12.refs_1_), channel_id=1, source_target_pairs={{0,2},{2,0},{1,3},{3,1},{4,6},{6,4},{5,7},{7,5},{8,10},{10,8},{9,1... | collective-permute-start | bytes 202760 | tf_op jit(solution)/shard_map/ppermute | solution.py:263
  32.7 4.9 %collective-permute-start.16 = (bf16[264,128]{1,0:T(8,128)(2,1)S(1)}, bf16[264,128]{1,0:T(8,128)(2,1)S(1)}, u32[]{:S(2)}, u32[]{:S(2)}) collective-permute-start(bf16[264,128]{1,0:T(8,128)(2,1)S(1)} %collective-permute-done.13.refs_2_), channel_id=1, source_target_pairs={{0,2},{2,0},{1,3},{3,1},{4,6},{6,4},{5,7},{7,5},{8,10},{10,8},{9,1... | collective-permute-start | bytes 202760 | tf_op jit(solution)/shard_map/ppermute | solution.py:263
  34.5 4.3 %collective-permute-start.11 = (bf16[264,128]{1,0:T(8,128)(2,1)S(1)}, bf16[264,128]{1,0:T(8,128)(2,1)S(1)}, u32[]{:S(2)}, u32[]{:S(2)}) collective-permute-start(bf16[264,128]{1,0:T(8,128)(2,1)S(1)} %collective-permute-done.10.refs_3_), channel_id=1, source_target_pairs={{0,2},{2,0},{1,3},{3,1},{4,6},{6,4},{5,7},{7,5},{8,10},{10,8},{9,1... | collective-permute-start | bytes 202760 | tf_op jit(solution)/shard_map/ppermute | solution.py:263
where the time goes:
time: 39.8 us; the launch traced here: 39.7 us
  starting transfers between devices  20.3 us (51%)
  waiting for transfers between devices  10.6 us (27%)
  Pallas kernels  7.33 us (18%)
  local copies, waits for them, and re-layouts  0.7 us (2%)
  between operations  0.7 us (2%)
    ppermute x6, starting transfers between devices, exchange(): arrived[step] = lax.ppermute(packets[step], 'sec', turn)  11.4 us
    ppermute x8, starting transfers between devices, exchange(): lax.ppermute(packet, 'op', turn)  8.24 us
    ppermute x8, waiting for transfers between devices, exchange(): lax.ppermute(packet, 'op', turn)  5.67 us
    ppermute x6, waiting for transfers between devices, exchange(): arrived[step] = lax.ppermute(packets[step], 'sec', turn)  3.37 us
    pallas_call x2, Pallas kernels, sigma_packets(): pl.pallas_call(functools.partial(product_kernel, is_first, split, paired,...  3.12 us
    pallas_call x4, Pallas kernels, call(): pl.pallas_call(kernel, out_shape=outs, in_specs=[whole(pltpu.VMEM)] * len...  2.11 us
    pallas_call x1, Pallas kernels, body(): pl.pallas_call(load_kernel, out_shape=[vec_bf16, jax.ShapeDtypeStruct(lef...  2.1 us
    ppermute x3, waiting for transfers between devices, from_others(): arrays.append(lax.ppermute(array, 'rep', turn))  1.54 us
  transfers between devices with their start and end apart: 17, of which 10 were waited for; matrix products, arithmetic and copies ran while one was open for 2% of the time, Pallas kernels for 8%

commit v1 on v0

--- a/solution.py
+++ b/solution.py
@@ -83,8 +83,8 @@
 
 
 def load_kernel(
-    psi_hbm, left_hbm, right_hbm, pairing_hbm, rows_hbm, cols_hbm, energy_hbm,
-    start_ref, left_ref, right_ref, list_ref, limit_ref, energy_ref, scalar_ref,
+    psi_hbm, left_hbm, pairing_hbm, rows_hbm, cols_hbm, energy_hbm,
+    start_ref, left_ref, list_ref, limit_ref, energy_ref, scalar_ref,
     psi_ref, level_ref, rows_ref, cols_ref, pairing_ref, entry_ref, count_ref, sems,
 ):
     sec_dev, half, width = psi_ref.shape
@@ -97,7 +97,6 @@
     ]
     for t in range(left_ref.shape[0]):
         pairs.append((left_hbm.at[t], left_ref.at[t]))
-        pairs.append((right_hbm.at[t], right_ref.at[t]))
     copies = [
         pltpu.make_async_copy(source, target, sems.at[i])
         for i, (source, target) in enumerate(pairs)
@@ -424,19 +423,18 @@
 
     psi_others = from_others(psi)
     level_others = from_others(energy)
-    start, left_env, right_env, lists, limits, levels, scalars = pl.pallas_call(
+    start, left_env, lists, limits, levels, scalars = pl.pallas_call(
         load_kernel,
         out_shape=[
             vec_bf16,
             jax.ShapeDtypeStruct(left_env.shape, BF16),
-            jax.ShapeDtypeStruct(right_env.shape, BF16),
             jax.ShapeDtypeStruct((sec_count, LANES), jnp.int32),
             jax.ShapeDtypeStruct((2 * sec_dev, LANES), jnp.int32),
             jax.ShapeDtypeStruct((sec_dev, half, LANES), F32),
             jax.ShapeDtypeStruct((16, width), F32),
         ],
-        in_specs=[whole(pltpu.HBM)] * 7,
-        out_specs=[whole(pltpu.VMEM)] * 7,
+        in_specs=[whole(pltpu.HBM)] * 6,
+        out_specs=[whole(pltpu.VMEM)] * 6,
         scratch_shapes=[
             pltpu.VMEM(vec_shape, BF16),
             pltpu.VMEM((sec_dev, half), F32),
@@ -445,13 +443,13 @@
             pltpu.SMEM((sec_dev, terms), jnp.int32),
             pltpu.SMEM((sec_count, LANES), jnp.int32),
             pltpu.SMEM((sec_count,), jnp.int32),
-            pltpu.SemaphoreType.DMA((6 + 2 * terms,)),
+            pltpu.SemaphoreType.DMA((6 + terms,)),
         ],
         compiler_params=params,
         name="load",
     )(*(
         pltpu.with_memory_space_constraint(array, pltpu.HBM)
-        for array in (psi, left_env, right_env, pairing.T, block_rows, block_cols, energy)
+        for array in (psi, left_env, pairing.T, block_rows, block_cols, energy)
     ))
 
     block_f32 = jax.ShapeDtypeStruct(vec_shape, F32)

time: 39.8 us -> 39.6 us (level)
  transfers between devices with their start and end apart: 17 -> 17, of which waited for: 10 -> 10; matrix products, arithmetic and copies ran while one was open for 2% -> 2% of each run, Pallas kernels for 8% -> 7%
where the time goes in v1:
time: 39.6 us; the launch traced here: 39.4 us
  starting transfers between devices  20.3 us (51%)
  waiting for transfers between devices  10.6 us (27%)
  Pallas kernels  7.06 us (18%)
  between operations  0.72 us (2%)
  local copies, waits for them, and re-layouts  0.71 us (2%)
    ppermute x6, starting transfers between devices, exchange(): arrived[step] = lax.ppermute(packets[step], 'sec', turn)  11.4 us
    ppermute x8, starting transfers between devices, exchange(): lax.ppermute(packet, 'op', turn)  8.25 us
    ppermute x8, waiting for transfers between devices, exchange(): lax.ppermute(packet, 'op', turn)  5.67 us
    ppermute x6, waiting for transfers between devices, exchange(): arrived[step] = lax.ppermute(packets[step], 'sec', turn)  3.39 us
    pallas_call x2, Pallas kernels, sigma_packets(): pl.pallas_call(functools.partial(product_kernel, is_first, split, paired,...  3.11 us
    pallas_call x4, Pallas kernels, call(): pl.pallas_call(kernel, out_shape=outs, in_specs=[whole(pltpu.VMEM)] * len...  2.11 us
    pallas_call x1, Pallas kernels, body(): pl.pallas_call(load_kernel, out_shape=[vec_bf16, jax.ShapeDtypeStruct(lef...  1.84 us
    ppermute x3, waiting for transfers between devices, from_others(): arrays.append(lax.ppermute(array, 'rep', turn))  1.54 us
  transfers between devices with their start and end apart: 17, of which 10 were waited for; matrix products, arithmetic and copies ran while one was open for 2% of the time, Pallas kernels for 7%

profile of v1, /device:TPU:0, one launch (start us, length us, event | category | flops | bytes accessed | tf_op | source)
XLA Modules:
  0.0 39.4 jit_solution(9197697495096974279)
XLA Ops:
  0.6 0.0 copy-start
  0.6 0.5 %collective-permute-start = (bf16[4,128,256]{2,1,0:T(8,128)(2,1)}, bf16[4,128,256]{2,1,0:T(8,128)(2,1)S(1)}, u32[]{:S(2)}, u32[]{:S(2)}) collective-permute-start(bf16[4,128,256]{2,1,0:T(8,128)(2,1)} %psi_hbm.1), channel_id=1, source_target_pairs={{1,0},{0,1},{3,2},{2,3},{5,4},{4,5},{7,6},{6,7},{9,8},{8,9},{11,10... | collective-permute-start | bytes 786440 | tf_op jit(solution)/shard_map/ppermute | solution.py:421
  1.2 0.1 collective-permute-start.1
  1.2 1.8 %load.1 = (bf16[4,128,256]{2,1,0:T(8,128)(2,1)S(1)}, bf16[8,4,128,256]{3,2,1,0:T(8,128)(2,1)S(1)}, s32[4,128]{1,0:T(4,128)S(1)}, s32[8,128]{1,0:T(8,128)S(1)}, f...) custom-call(bf16[4,128,256]{2,1,0:T(8,128)(2,1)} %psi_hbm.1, bf16[8,4,128,256]{3,2,1,0:T(8,128)(2,1)} %left_hbm.1, ...), custom_call_target="tpu_custom_call" | custom-call | tf_op jit(solution)/shard_map/load/pallas_call | solution.py:426
  3.1 0.0 collective-permute-done.1.refs_7_
  3.1 0.0 collective-permute-done.refs_6_
  3.1 0.0 copy-done
  3.1 1.6 %products_first.1 = (bf16[264,128]{1,0:T(8,128)(2,1)S(1)}, bf16[264,128]{1,0:T(8,128)(2,1)S(1)}, bf16[264,128]{1,0:T(8,128)(2,1)S(1)}, bf16[264,128]{1,0:T(8,128)(2,1)S(1)}) custom-call(s32[4,128]{1,0:T(4,128)S(1)} %get-tuple-element.23.refs_0_, bf16[8,4,128,256]{3,2,1,0:T(8,128)(2,1)S(1)} %get-tuple-element.24.refs_1_, bf16[8,256,256]{2,1,0:T(8,128)(2,1)S(1)} %copy-done, ...), custom_call_target="tpu_custom_call" | custom-call | flops 1073741824 | bytes 3145728 | tf_op jit(solution)/shard_map/products_first/pallas_call | solution.py:236
  4.7 3.0 %collective-permute-start.4 = (bf16[264,128]{1,0:T(8,128)(2,1)S(1)}, bf16[264,128]{1,0:T(8,128)(2,1)S(1)}, u32[]{:S(2)}, u32[]{:S(2)}) collective-permute-start(bf16[264,128]{1,0:T(8,128)(2,1)S(1)} %get-tuple-element.30), channel_id=1, source_target_pairs={{0,4},{4,8},{8,12},{12,0},{1,5},{5,9},{9,13},{13,1},{2,6},{6,10},{... | collective-permute-start | bytes 202760 | tf_op jit(solution)/shard_map/ppermute | solution.py:273
  7.8 2.6 %collective-permute-start.5 = (bf16[264,128]{1,0:T(8,128)(2,1)S(1)}, bf16[264,128]{1,0:T(8,128)(2,1)S(1)}, u32[]{:S(2)}, u32[]{:S(2)}) collective-permute-start(bf16[264,128]{1,0:T(8,128)(2,1)S(1)} %get-tuple-element.31), channel_id=1, source_target_pairs={{0,8},{4,12},{8,0},{12,4},{1,9},{5,13},{9,1},{13,5},{2,10},{6,14},... | collective-permute-start | bytes 202760 | tf_op jit(solution)/shard_map/ppermute | solution.py:273
  10.3 1.3 %collective-permute-start.2 = (bf16[264,128]{1,0:T(8,128)(2,1)S(1)}, bf16[264,128]{1,0:T(8,128)(2,1)S(1)}, u32[]{:S(2)}, u32[]{:S(2)}) collective-permute-start(bf16[264,128]{1,0:T(8,128)(2,1)S(1)} %get-tuple-element.28), channel_id=1, source_target_pairs={{0,12},{4,0},{8,4},{12,8},{1,13},{5,1},{9,5},{13,9},{2,14},{6,2},{... | collective-permute-start | bytes 202760 | tf_op jit(solution)/shard_map/ppermute | solution.py:273
  11.7 1.5 %collective-permute-start.6 = (bf16[264,128]{1,0:T(8,128)(2,1)S(1)}, bf16[264,128]{1,0:T(8,128)(2,1)S(1)}, u32[]{:S(2)}, u32[]{:S(2)}) collective-permute-start(bf16[264,128]{1,0:T(8,128)(2,1)S(1)} %get-tuple-element.29.refs_0_), channel_id=1, source_target_pairs={{0,2},{2,0},{1,3},{3,1},{4,6},{6,4},{5,7},{7,5},{8,10},{10,8},{9,1... | collective-permute-start | bytes 202760 | tf_op jit(solution)/shard_map/ppermute | solution.py:262
  13.2 0.0 collective-permute-done.4.refs_1_
  13.2 0.8 %collective-permute-start.7 = (bf16[264,128]{1,0:T(8,128)(2,1)S(1)}, bf16[264,128]{1,0:T(8,128)(2,1)S(1)}, u32[]{:S(2)}, u32[]{:S(2)}) collective-permute-start(bf16[264,128]{1,0:T(8,128)(2,1)S(1)} %collective-permute-done.4.refs_1_), channel_id=1, source_target_pairs={{0,2},{2,0},{1,3},{3,1},{4,6},{6,4},{5,7},{7,5},{8,10},{10,8},{9,1... | collective-permute-start | bytes 202760 | tf_op jit(solution)/shard_map/ppermute | solution.py:262
  14.0 1.1 %collective-permute-done.5.refs_2_ = bf16[264,128]{1,0:T(8,128)(2,1)S(1)} collective-permute-done((bf16[264,128]{1,0:T(8,128)(2,1)S(1)}, bf16[264,128]{1,0:T(8,128)(2,1)S(1)}, u32[]{:S(2)}, u32[]{:S(2)}) %collective-permute-start.5) | collective-permute-done | bytes 67616 | tf_op jit(solution)/shard_map/ppermute | solution.py:273
  15.2 1.5 %collective-permute-start.8 = (bf16[264,128]{1,0:T(8,128)(2,1)S(1)}, bf16[264,128]{1,0:T(8,128)(2,1)S(1)}, u32[]{:S(2)}, u32[]{:S(2)}) collective-permute-start(bf16[264,128]{1,0:T(8,128)(2,1)S(1)} %collective-permute-done.5.refs_2_), channel_id=1, source_target_pairs={{0,2},{2,0},{1,3},{3,1},{4,6},{6,4},{5,7},{7,5},{8,10},{10,8},{9,1... | collective-permute-start | bytes 202760 | tf_op jit(solution)/shard_map/ppermute | solution.py:262
  16.7 0.0 collective-permute-done.2.refs_3_
  16.7 0.5 %collective-permute-start.3 = (bf16[264,128]{1,0:T(8,128)(2,1)S(1)}, bf16[264,128]{1,0:T(8,128)(2,1)S(1)}, u32[]{:S(2)}, u32[]{:S(2)}) collective-permute-start(bf16[264,128]{1,0:T(8,128)(2,1)S(1)} %collective-permute-done.2.refs_3_), channel_id=1, source_target_pairs={{0,2},{2,0},{1,3},{3,1},{4,6},{6,4},{5,7},{7,5},{8,10},{10,8},{9,1... | collective-permute-start | bytes 202760 | tf_op jit(solution)/shard_map/ppermute | solution.py:262
  17.2 0.0 collective-permute-done.6.refs_4_
  17.2 0.3 collective-permute-done.7.refs_5_
  17.5 2.5 %collective-permute-done.8.refs_6_ = bf16[264,128]{1,0:T(8,128)(2,1)S(1)} collective-permute-done((bf16[264,128]{1,0:T(8,128)(2,1)S(1)}, bf16[264,128]{1,0:T(8,128)(2,1)S(1)}, u32[]{:S(2)}, u32[]{:S(2)}) %collective-permute-start.8) | collective-permute-done | bytes 67616 | tf_op jit(solution)/shard_map/ppermute | solution.py:262
  20.0 0.4 %combine_first_early.1 = (f32[4,128,256]{2,1,0:T(8,128)S(1)}, f32[8,128]{1,0:T(8,128)S(1)}) custom-call(bf16[264,128]{1,0:T(8,128)(2,1)S(1)} %get-tuple-element.29.refs_0_, bf16[264,128]{1,0:T(8,128)(2,1)S(1)} %collective-permute-done.4.refs_1_, bf16[264,128]{1,0:T(8,128)(2,1)S(1)} %collective-permute-done.5.refs_2_, ...), custom_call_target="tpu_custom_call" | custom-call | tf_op jit(solution)/shard_map/combine_first_early/pallas_call | solution.py:392
  20.4 0.5 %collective-permute-done.3.refs_0_ = bf16[264,128]{1,0:T(8,128)(2,1)S(1)} collective-permute-done((bf16[264,128]{1,0:T(8,128)(2,1)S(1)}, bf16[264,128]{1,0:T(8,128)(2,1)S(1)}, u32[]{:S(2)}, u32[]{:S(2)}) %collective-permute-start.3) | collective-permute-done | bytes 67616 | tf_op jit(solution)/shard_map/ppermute | solution.py:262
  20.9 0.4 combine_first.1
  21.3 0.1 collective-permute-start.9
  21.4 1.5 %collective-permute-done.9.refs_4_ = bf16[528,256]{1,0:T(8,128)(2,1)S(1)} collective-permute-done((bf16[528,256]{1,0:T(8,128)(2,1)S(1)}, bf16[528,256]{1,0:T(8,128)(2,1)S(1)}, u32[]{:S(2)}, u32[]{:S(2)}) %collective-permute-start.9) | collective-permute-done | bytes 270368 | tf_op jit(solution)/shard_map/ppermute | solution.py:421
  22.9 1.5 %products_second.1 = (bf16[264,128]{1,0:T(8,128)(2,1)S(1)}, bf16[264,128]{1,0:T(8,128)(2,1)S(1)}, bf16[264,128]{1,0:T(8,128)(2,1)S(1)}, bf16[264,128]{1,0:T(8,128)(2,1)S(1)}) custom-call(s32[4,128]{1,0:T(4,128)S(1)} %get-tuple-element.23.refs_0_, bf16[8,4,128,256]{3,2,1,0:T(8,128)(2,1)S(1)} %get-tuple-element.24.refs_1_, bf16[8,256,256]{2,1,0:T(8,128)(2,1)S(1)} %copy-done, ...), custom_call_target="tpu_custom_call" | custom-call | flops 1073741824 | bytes 3145728 | tf_op jit(solution)/shard_map/products_second/pallas_call | solution.py:236
  24.4 1.1 %collective-permute-start.12 = (bf16[264,128]{1,0:T(8,128)(2,1)S(1)}, bf16[264,128]{1,0:T(8,128)(2,1)S(1)}, u32[]{:S(2)}, u32[]{:S(2)}) collective-permute-start(bf16[264,128]{1,0:T(8,128)(2,1)S(1)} %get-tuple-element.39), channel_id=1, source_target_pairs={{0,8},{4,12},{8,0},{12,4},{1,9},{5,13},{9,1},{13,5},{2,10},{6,14},... | collective-permute-start | bytes 202760 | tf_op jit(solution)/shard_map/ppermute | solution.py:273
  25.5 2.7 %collective-permute-start.13 = (bf16[264,128]{1,0:T(8,128)(2,1)S(1)}, bf16[264,128]{1,0:T(8,128)(2,1)S(1)}, u32[]{:S(2)}, u32[]{:S(2)}) collective-permute-start(bf16[264,128]{1,0:T(8,128)(2,1)S(1)} %get-tuple-element.40), channel_id=1, source_target_pairs={{0,4},{4,0},{8,12},{12,8},{1,5},{5,1},{9,13},{13,9},{2,6},{6,2},{1... | collective-permute-start | bytes 202760 | tf_op jit(solution)/shard_map/ppermute | solution.py:273
  28.2 0.7 %collective-permute-start.10 = (bf16[264,128]{1,0:T(8,128)(2,1)S(1)}, bf16[264,128]{1,0:T(8,128)(2,1)S(1)}, u32[]{:S(2)}, u32[]{:S(2)}) collective-permute-start(bf16[264,128]{1,0:T(8,128)(2,1)S(1)} %get-tuple-element.37), channel_id=1, source_target_pairs={{0,12},{4,8},{8,4},{12,0},{1,13},{5,9},{9,5},{13,1},{2,14},{6,10},... | collective-permute-start | bytes 202760 | tf_op jit(solution)/shard_map/ppermute | solution.py:273
  28.9 1.1 %collective-permute-start.14 = (bf16[264,128]{1,0:T(8,128)(2,1)S(1)}, bf16[264,128]{1,0:T(8,128)(2,1)S(1)}, u32[]{:S(2)}, u32[]{:S(2)}) collective-permute-start(bf16[264,128]{1,0:T(8,128)(2,1)S(1)} %get-tuple-element.38.refs_0_), channel_id=1, source_target_pairs={{0,2},{2,0},{1,3},{3,1},{4,6},{6,4},{5,7},{7,5},{8,10},{10,8},{9,1... | collective-permute-start | bytes 202760 | tf_op jit(solution)/shard_map/ppermute | solution.py:262
  30.0 1.6 %collective-permute-done.12.refs_1_ = bf16[264,128]{1,0:T(8,128)(2,1)S(1)} collective-permute-done((bf16[264,128]{1,0:T(8,128)(2,1)S(1)}, bf16[264,128]{1,0:T(8,128)(2,1)S(1)}, u32[]{:S(2)}, u32[]{:S(2)}) %collective-permute-start.12) | collective-permute-done | bytes 67616 | tf_op jit(solution)/shard_map/ppermute | solution.py:273
  31.6 0.9 %collective-permute-start.15 = (bf16[264,128]{1,0:T(8,128)(2,1)S(1)}, bf16[264,128]{1,0:T(8,128)(2,1)S(1)}, u32[]{:S(2)}, u32[]{:S(2)}) collective-permute-start(bf16[264,128]{1,0:T(8,128)(2,1)S(1)} %collective-permute-done.12.refs_1_), channel_id=1, source_target_pairs={{0,2},{2,0},{1,3},{3,1},{4,6},{6,4},{5,7},{7,5},{8,10},{10,8},{9,1... | collective-permute-start | bytes 202760 | tf_op jit(solution)/shard_map/ppermute | solution.py:262
  32.5 0.0 collective-permute-done.13.refs_2_
  32.5 1.2 %collective-permute-start.16 = (bf16[264,128]{1,0:T(8,128)(2,1)S(1)}, bf16[264,128]{1,0:T(8,128)(2,1)S(1)}, u32[]{:S(2)}, u32[]{:S(2)}) collective-permute-start(bf16[264,128]{1,0:T(8,128)(2,1)S(1)} %collective-permute-done.13.refs_2_), channel_id=1, source_target_pairs={{0,2},{2,0},{1,3},{3,1},{4,6},{6,4},{5,7},{7,5},{8,10},{10,8},{9,1... | collective-permute-start | bytes 202760 | tf_op jit(solution)/shard_map/ppermute | solution.py:262
  33.6 0.7 %collective-permute-done.10.refs_3_ = bf16[264,128]{1,0:T(8,128)(2,1)S(1)} collective-permute-done((bf16[264,128]{1,0:T(8,128)(2,1)S(1)}, bf16[264,128]{1,0:T(8,128)(2,1)S(1)}, u32[]{:S(2)}, u32[]{:S(2)}) %collective-permute-start.10) | collective-permute-done | bytes 67616 | tf_op jit(solution)/shard_map/ppermute | solution.py:273
  34.3 0.7 %collective-permute-start.11 = (bf16[264,128]{1,0:T(8,128)(2,1)S(1)}, bf16[264,128]{1,0:T(8,128)(2,1)S(1)}, u32[]{:S(2)}, u32[]{:S(2)}) collective-permute-start(bf16[264,128]{1,0:T(8,128)(2,1)S(1)} %collective-permute-done.10.refs_3_), channel_id=1, source_target_pairs={{0,2},{2,0},{1,3},{3,1},{4,6},{6,4},{5,7},{7,5},{8,10},{10,8},{9,1... | collective-permute-start | bytes 202760 | tf_op jit(solution)/shard_map/ppermute | solution.py:262
  35.0 0.7 %copy.9 = bf16[4,128,256]{2,1,0:T(8,128)(2,1)} copy(bf16[4,128,256]{2,1,0:T(8,128)(2,1)S(1)} %get-tuple-element.44) | data formatting | bytes 524288
  35.7 0.0 collective-permute-done.14.refs_4_
  35.8 0.6 %collective-permute-done.15.refs_5_ = bf16[264,128]{1,0:T(8,128)(2,1)S(1)} collective-permute-done((bf16[264,128]{1,0:T(8,128)(2,1)S(1)}, bf16[264,128]{1,0:T(8,128)(2,1)S(1)}, u32[]{:S(2)}, u32[]{:S(2)}) %collective-permute-start.15) | collective-permute-done | bytes 67616 | tf_op jit(solution)/shard_map/ppermute | solution.py:262
  36.4 1.0 %collective-permute-done.16.refs_6_ = bf16[264,128]{1,0:T(8,128)(2,1)S(1)} collective-permute-done((bf16[264,128]{1,0:T(8,128)(2,1)S(1)}, bf16[264,128]{1,0:T(8,128)(2,1)S(1)}, u32[]{:S(2)}, u32[]{:S(2)}) %collective-permute-start.16) | collective-permute-done | bytes 67616 | tf_op jit(solution)/shard_map/ppermute | solution.py:262
  37.3 0.5 %combine_second_early.1 = (f32[4,128,256]{2,1,0:T(8,128)S(1)}, f32[8,128]{1,0:T(8,128)S(1)}) custom-call(bf16[264,128]{1,0:T(8,128)(2,1)S(1)} %get-tuple-element.38.refs_0_, bf16[264,128]{1,0:T(8,128)(2,1)S(1)} %collective-permute-done.12.refs_1_, bf16[264,128]{1,0:T(8,128)(2,1)S(1)} %collective-permute-done.13.refs_2_, ...), custom_call_target="tpu_custom_call" | custom-call | tf_op jit(solution)/shard_map/combine_second_early/pallas_call | solution.py:392
  37.8 0.7 %collective-permute-done.11.refs_0_ = bf16[264,128]{1,0:T(8,128)(2,1)S(1)} collective-permute-done((bf16[264,128]{1,0:T(8,128)(2,1)S(1)}, bf16[264,128]{1,0:T(8,128)(2,1)S(1)}, u32[]{:S(2)}, u32[]{:S(2)}) %collective-permute-start.11) | collective-permute-done | bytes 67616 | tf_op jit(solution)/shard_map/ppermute | solution.py:262
  38.6 0.8 %combine_second.1 = bf16[4,128,256]{2,1,0:T(8,128)(2,1)} custom-call(bf16[264,128]{1,0:T(8,128)(2,1)S(1)} %collective-permute-done.11.refs_0_, s32[8,128]{1,0:T(8,128)S(1)} %get-tuple-element.26.refs_4_.refs_1_, f32[4,128,256]{2,1,0:T(8,128)S(1)} %get-tuple-element.42.refs_2_, f32[8,128]{1,0:T(8,128)S(1)} %get-tuple-element.43.refs_3_), custom_call_target="tpu_custom_call" | custom-call | tf_op jit(solution)/shard_map/combine_second/pallas_call | solution.py:392
Async XLA Ops:
  0.6 2.5 %copy-start = (bf16[8,256,256]{2,1,0:T(8,128)(2,1)S(1)}, bf16[8,256,256]{2,1,0:T(8,128)(2,1)}, u32[]{:S(2)}) copy-start(bf16[8,256,256]{2,1,0:T(8,128)(2,1)} %refs_2_.3) | copy-start | bytes 3145732
  0.6 2.5 %collective-permute-start = (bf16[4,128,256]{2,1,0:T(8,128)(2,1)}, bf16[4,128,256]{2,1,0:T(8,128)(2,1)S(1)}, u32[]{:S(2)}, u32[]{:S(2)}) collective-permute-start(bf16[4,128,256]{2,1,0:T(8,128)(2,1)} %psi_hbm.1), channel_id=1, source_target_pairs={{1,0},{0,1},{3,2},{2,3},{5,4},{4,5},{7,6},{6,7},{9,8},{8,9},{11,10... | collective-permute-start | bytes 786440 | tf_op jit(solution)/shard_map/ppermute | solution.py:421
  1.2 1.9 %collective-permute-start.1 = (f32[4,128]{1,0:T(4,128)}, f32[4,128]{1,0:T(4,128)S(1)}, u32[]{:S(2)}, u32[]{:S(2)}) collective-permute-start(f32[4,128]{1,0:T(4,128)} %energy_hbm.1), channel_id=1, source_target_pairs={{1,0},{0,1},{3,2},{2,3},{5,4},{4,5},{7,6},{6,7},{9,8},{8,9},{11,10... | collective-permute-start | bytes 6152 | tf_op jit(solution)/shard_map/ppermute | solution.py:421
  4.7 8.5 %collective-permute-start.4 = (bf16[264,128]{1,0:T(8,128)(2,1)S(1)}, bf16[264,128]{1,0:T(8,128)(2,1)S(1)}, u32[]{:S(2)}, u32[]{:S(2)}) collective-permute-start(bf16[264,128]{1,0:T(8,128)(2,1)S(1)} %get-tuple-element.30), channel_id=1, source_target_pairs={{0,4},{4,8},{8,12},{12,0},{1,5},{5,9},{9,13},{13,1},{2,6},{6,10},{... | collective-permute-start | bytes 202760 | tf_op jit(solution)/shard_map/ppermute | solution.py:273
  7.8 7.4 %collective-permute-start.5 = (bf16[264,128]{1,0:T(8,128)(2,1)S(1)}, bf16[264,128]{1,0:T(8,128)(2,1)S(1)}, u32[]{:S(2)}, u32[]{:S(2)}) collective-permute-start(bf16[264,128]{1,0:T(8,128)(2,1)S(1)} %get-tuple-element.31), channel_id=1, source_target_pairs={{0,8},{4,12},{8,0},{12,4},{1,9},{5,13},{9,1},{13,5},{2,10},{6,14},... | collective-permute-start | bytes 202760 | tf_op jit(solution)/shard_map/ppermute | solution.py:273
  10.3 6.3 %collective-permute-start.2 = (bf16[264,128]{1,0:T(8,128)(2,1)S(1)}, bf16[264,128]{1,0:T(8,128)(2,1)S(1)}, u32[]{:S(2)}, u32[]{:S(2)}) collective-permute-start(bf16[264,128]{1,0:T(8,128)(2,1)S(1)} %get-tuple-element.28), channel_id=1, source_target_pairs={{0,12},{4,0},{8,4},{12,8},{1,13},{5,1},{9,5},{13,9},{2,14},{6,2},{... | collective-permute-start | bytes 202760 | tf_op jit(solution)/shard_map/ppermute | solution.py:273
  11.7 5.5 %collective-permute-start.6 = (bf16[264,128]{1,0:T(8,128)(2,1)S(1)}, bf16[264,128]{1,0:T(8,128)(2,1)S(1)}, u32[]{:S(2)}, u32[]{:S(2)}) collective-permute-start(bf16[264,128]{1,0:T(8,128)(2,1)S(1)} %get-tuple-element.29.refs_0_), channel_id=1, source_target_pairs={{0,2},{2,0},{1,3},{3,1},{4,6},{6,4},{5,7},{7,5},{8,10},{10,8},{9,1... | collective-permute-start | bytes 202760 | tf_op jit(solution)/shard_map/ppermute | solution.py:262
  13.2 4.3 %collective-permute-start.7 = (bf16[264,128]{1,0:T(8,128)(2,1)S(1)}, bf16[264,128]{1,0:T(8,128)(2,1)S(1)}, u32[]{:S(2)}, u32[]{:S(2)}) collective-permute-start(bf16[264,128]{1,0:T(8,128)(2,1)S(1)} %collective-permute-done.4.refs_1_), channel_id=1, source_target_pairs={{0,2},{2,0},{1,3},{3,1},{4,6},{6,4},{5,7},{7,5},{8,10},{10,8},{9,1... | collective-permute-start | bytes 202760 | tf_op jit(solution)/shard_map/ppermute | solution.py:262
  15.2 4.8 %collective-permute-start.8 = (bf16[264,128]{1,0:T(8,128)(2,1)S(1)}, bf16[264,128]{1,0:T(8,128)(2,1)S(1)}, u32[]{:S(2)}, u32[]{:S(2)}) collective-permute-start(bf16[264,128]{1,0:T(8,128)(2,1)S(1)} %collective-permute-done.5.refs_2_), channel_id=1, source_target_pairs={{0,2},{2,0},{1,3},{3,1},{4,6},{6,4},{5,7},{7,5},{8,10},{10,8},{9,1... | collective-permute-start | bytes 202760 | tf_op jit(solution)/shard_map/ppermute | solution.py:262
  16.7 4.3 %collective-permute-start.3 = (bf16[264,128]{1,0:T(8,128)(2,1)S(1)}, bf16[264,128]{1,0:T(8,128)(2,1)S(1)}, u32[]{:S(2)}, u32[]{:S(2)}) collective-permute-start(bf16[264,128]{1,0:T(8,128)(2,1)S(1)} %collective-permute-done.2.refs_3_), channel_id=1, source_target_pairs={{0,2},{2,0},{1,3},{3,1},{4,6},{6,4},{5,7},{7,5},{8,10},{10,8},{9,1... | collective-permute-start | bytes 202760 | tf_op jit(solution)/shard_map/ppermute | solution.py:262
  21.3 1.6 %collective-permute-start.9 = (bf16[528,256]{1,0:T(8,128)(2,1)S(1)}, bf16[528,256]{1,0:T(8,128)(2,1)S(1)}, u32[]{:S(2)}, u32[]{:S(2)}) collective-permute-start(bf16[528,256]{1,0:T(8,128)(2,1)S(1)} %get-tuple-element.36.refs_3_.refs_7_), channel_id=1, source_target_pairs={{1,0},{0,1},{3,2},{2,3},{5,4},{4,5},{7,6},{6,7},{9,8},{8,9},{11,10... | collective-permute-start | bytes 811016 | tf_op jit(solution)/shard_map/ppermute | solution.py:421
  24.4 7.2 %collective-permute-start.12 = (bf16[264,128]{1,0:T(8,128)(2,1)S(1)}, bf16[264,128]{1,0:T(8,128)(2,1)S(1)}, u32[]{:S(2)}, u32[]{:S(2)}) collective-permute-start(bf16[264,128]{1,0:T(8,128)(2,1)S(1)} %get-tuple-element.39), channel_id=1, source_target_pairs={{0,8},{4,12},{8,0},{12,4},{1,9},{5,13},{9,1},{13,5},{2,10},{6,14},... | collective-permute-start | bytes 202760 | tf_op jit(solution)/shard_map/ppermute | solution.py:273
  25.5 7.0 %collective-permute-start.13 = (bf16[264,128]{1,0:T(8,128)(2,1)S(1)}, bf16[264,128]{1,0:T(8,128)(2,1)S(1)}, u32[]{:S(2)}, u32[]{:S(2)}) collective-permute-start(bf16[264,128]{1,0:T(8,128)(2,1)S(1)} %get-tuple-element.40), channel_id=1, source_target_pairs={{0,4},{4,0},{8,12},{12,8},{1,5},{5,1},{9,13},{13,9},{2,6},{6,2},{1... | collective-permute-start | bytes 202760 | tf_op jit(solution)/shard_map/ppermute | solution.py:273
  28.2 6.1 %collective-permute-start.10 = (bf16[264,128]{1,0:T(8,128)(2,1)S(1)}, bf16[264,128]{1,0:T(8,128)(2,1)S(1)}, u32[]{:S(2)}, u32[]{:S(2)}) collective-permute-start(bf16[264,128]{1,0:T(8,128)(2,1)S(1)} %get-tuple-element.37), channel_id=1, source_target_pairs={{0,12},{4,8},{8,4},{12,0},{1,13},{5,9},{9,5},{13,1},{2,14},{6,10},... | collective-permute-start | bytes 202760 | tf_op jit(solution)/shard_map/ppermute | solution.py:273
  28.9 6.9 %collective-permute-start.14 = (bf16[264,128]{1,0:T(8,128)(2,1)S(1)}, bf16[264,128]{1,0:T(8,128)(2,1)S(1)}, u32[]{:S(2)}, u32[]{:S(2)}) collective-permute-start(bf16[264,128]{1,0:T(8,128)(2,1)S(1)} %get-tuple-element.38.refs_0_), channel_id=1, source_target_pairs={{0,2},{2,0},{1,3},{3,1},{4,6},{6,4},{5,7},{7,5},{8,10},{10,8},{9,1... | collective-permute-start | bytes 202760 | tf_op jit(solution)/shard_map/ppermute | solution.py:262
  31.6 4.8 %collective-permute-start.15 = (bf16[264,128]{1,0:T(8,128)(2,1)S(1)}, bf16[264,128]{1,0:T(8,128)(2,1)S(1)}, u32[]{:S(2)}, u32[]{:S(2)}) collective-permute-start(bf16[264,128]{1,0:T(8,128)(2,1)S(1)} %collective-permute-done.12.refs_1_), channel_id=1, source_target_pairs={{0,2},{2,0},{1,3},{3,1},{4,6},{6,4},{5,7},{7,5},{8,10},{10,8},{9,1... | collective-permute-start | bytes 202760 | tf_op jit(solution)/shard_map/ppermute | solution.py:262
  32.5 4.9 %collective-permute-start.16 = (bf16[264,128]{1,0:T(8,128)(2,1)S(1)}, bf16[264,128]{1,0:T(8,128)(2,1)S(1)}, u32[]{:S(2)}, u32[]{:S(2)}) collective-permute-start(bf16[264,128]{1,0:T(8,128)(2,1)S(1)} %collective-permute-done.13.refs_2_), channel_id=1, source_target_pairs={{0,2},{2,0},{1,3},{3,1},{4,6},{6,4},{5,7},{7,5},{8,10},{10,8},{9,1... | collective-permute-start | bytes 202760 | tf_op jit(solution)/shard_map/ppermute | solution.py:262
  34.3 4.3 %collective-permute-start.11 = (bf16[264,128]{1,0:T(8,128)(2,1)S(1)}, bf16[264,128]{1,0:T(8,128)(2,1)S(1)}, u32[]{:S(2)}, u32[]{:S(2)}) collective-permute-start(bf16[264,128]{1,0:T(8,128)(2,1)S(1)} %collective-permute-done.10.refs_3_), channel_id=1, source_target_pairs={{0,2},{2,0},{1,3},{3,1},{4,6},{6,4},{5,7},{7,5},{8,10},{10,8},{9,1... | collective-permute-start | bytes 202760 | tf_op jit(solution)/shard_map/ppermute | solution.py:262

commit v2 on v1

--- a/solution.py
+++ b/solution.py
@@ -202,6 +202,14 @@
     else:
         head = sum(ref[sec_dev * half:].astype(F32) for ref in vector_refs)
         scalars = [head_scalar(head, i)[:, :LANES] for i in range(2)]
+    for t in range(terms):
+        block = pl.ds(t * sec_dev, sec_dev)
+        outer = jnp.dot(
+            inner_ref[block].reshape(sec_dev * half, width),
+            right_ref[t],
+            preferred_element_type=F32,
+        )
+        inner_ref[block] = outer.astype(BF16).reshape(sec_dev, half, width)
     fetch.wait()
     for d in range(sec_count):
         if not split:
@@ -212,9 +220,7 @@
             owner = remainder(sec + d, sec_count)
         packet = jnp.zeros((half, width), F32)
         for i in range(cap):
-            pair = entry_ref[owner, i]
-            term = jnp.minimum(quotient(pair, sec_dev), terms - 1)
-            packet += jnp.dot(inner_ref[pair], right_ref[term], preferred_element_type=F32)
+            packet += inner_ref[entry_ref[owner, i]].astype(F32)
         out = out_refs[d] if split else out_refs[0].at[d]
         for column in range(width // LANES):
             out[column * half:(column + 1) * half, :] = packet[

time: 39.6 us -> 39.7 us (level)
  no operation moved by 1% of the time
where the time goes in v2:
time: 39.7 us; the launch traced here: 39.6 us
  starting transfers between devices  20.3 us (51%)
  waiting for transfers between devices  10.6 us (27%)
  Pallas kernels  7.21 us (18%)
  between operations  0.72 us (2%)
  local copies, waits for them, and re-layouts  0.71 us (2%)
    ppermute x6, starting transfers between devices, exchange(): arrived[step] = lax.ppermute(packets[step], 'sec', turn)  11.4 us
    ppermute x8, starting transfers between devices, exchange(): lax.ppermute(packet, 'op', turn)  8.23 us
    ppermute x8, waiting for transfers between devices, exchange(): lax.ppermute(packet, 'op', turn)  5.67 us
    ppermute x6, waiting for transfers between devices, exchange(): arrived[step] = lax.ppermute(packets[step], 'sec', turn)  3.39 us
    pallas_call x2, Pallas kernels, sigma_packets(): pl.pallas_call(functools.partial(product_kernel, is_first, split, paired,...  3.25 us
    pallas_call x4, Pallas kernels, call(): pl.pallas_call(kernel, out_shape=outs, in_specs=[whole(pltpu.VMEM)] * len...  2.11 us
    pallas_call x1, Pallas kernels, body(): pl.pallas_call(load_kernel, out_shape=[vec_bf16, jax.ShapeDtypeStruct(lef...  1.84 us
    ppermute x3, waiting for transfers between devices, from_others(): arrays.append(lax.ppermute(array, 'rep', turn))  1.54 us
  transfers between devices with their start and end apart: 17, of which 10 were waited for; matrix products, arithmetic and copies ran while one was open for 2% of the time, Pallas kernels for 7%

profile of v2, /device:TPU:0, one launch (start us, length us, event | category | flops | bytes accessed | tf_op | source)
XLA Modules:
  0.0 39.6 jit_solution(10853295820674138006)
XLA Ops:
  0.6 0.0 copy-start
  0.6 0.5 %collective-permute-start = (bf16[4,128,256]{2,1,0:T(8,128)(2,1)}, bf16[4,128,256]{2,1,0:T(8,128)(2,1)S(1)}, u32[]{:S(2)}, u32[]{:S(2)}) collective-permute-start(bf16[4,128,256]{2,1,0:T(8,128)(2,1)} %psi_hbm.1), channel_id=1, source_target_pairs={{1,0},{0,1},{3,2},{2,3},{5,4},{4,5},{7,6},{6,7},{9,8},{8,9},{11,10... | collective-permute-start | bytes 786440 | tf_op jit(solution)/shard_map/ppermute | solution.py:427
  1.2 0.1 collective-permute-start.1
  1.2 1.8 %load.1 = (bf16[4,128,256]{2,1,0:T(8,128)(2,1)S(1)}, bf16[8,4,128,256]{3,2,1,0:T(8,128)(2,1)S(1)}, s32[4,128]{1,0:T(4,128)S(1)}, s32[8,128]{1,0:T(8,128)S(1)}, f...) custom-call(bf16[4,128,256]{2,1,0:T(8,128)(2,1)} %psi_hbm.1, bf16[8,4,128,256]{3,2,1,0:T(8,128)(2,1)} %left_hbm.1, ...), custom_call_target="tpu_custom_call" | custom-call | tf_op jit(solution)/shard_map/load/pallas_call | solution.py:432
  3.1 0.0 collective-permute-done.1.refs_7_
  3.1 0.0 collective-permute-done.refs_6_
  3.1 0.0 copy-done
  3.1 1.6 %products_first.1 = (bf16[264,128]{1,0:T(8,128)(2,1)S(1)}, bf16[264,128]{1,0:T(8,128)(2,1)S(1)}, bf16[264,128]{1,0:T(8,128)(2,1)S(1)}, bf16[264,128]{1,0:T(8,128)(2,1)S(1)}) custom-call(s32[4,128]{1,0:T(4,128)S(1)} %get-tuple-element.23.refs_0_, bf16[8,4,128,256]{3,2,1,0:T(8,128)(2,1)S(1)} %get-tuple-element.24.refs_1_, bf16[8,256,256]{2,1,0:T(8,128)(2,1)S(1)} %copy-done, ...), custom_call_target="tpu_custom_call" | custom-call | flops 1073741824 | bytes 3145728 | tf_op jit(solution)/shard_map/products_first/pallas_call | solution.py:242
  4.8 3.1 %collective-permute-start.4 = (bf16[264,128]{1,0:T(8,128)(2,1)S(1)}, bf16[264,128]{1,0:T(8,128)(2,1)S(1)}, u32[]{:S(2)}, u32[]{:S(2)}) collective-permute-start(bf16[264,128]{1,0:T(8,128)(2,1)S(1)} %get-tuple-element.30), channel_id=1, source_target_pairs={{0,4},{4,8},{8,12},{12,0},{1,5},{5,9},{9,13},{13,1},{2,6},{6,10},{... | collective-permute-start | bytes 202760 | tf_op jit(solution)/shard_map/ppermute | solution.py:279
  7.8 2.6 %collective-permute-start.5 = (bf16[264,128]{1,0:T(8,128)(2,1)S(1)}, bf16[264,128]{1,0:T(8,128)(2,1)S(1)}, u32[]{:S(2)}, u32[]{:S(2)}) collective-permute-start(bf16[264,128]{1,0:T(8,128)(2,1)S(1)} %get-tuple-element.31), channel_id=1, source_target_pairs={{0,8},{4,12},{8,0},{12,4},{1,9},{5,13},{9,1},{13,5},{2,10},{6,14},... | collective-permute-start | bytes 202760 | tf_op jit(solution)/shard_map/ppermute | solution.py:279
  10.4 1.3 %collective-permute-start.2 = (bf16[264,128]{1,0:T(8,128)(2,1)S(1)}, bf16[264,128]{1,0:T(8,128)(2,1)S(1)}, u32[]{:S(2)}, u32[]{:S(2)}) collective-permute-start(bf16[264,128]{1,0:T(8,128)(2,1)S(1)} %get-tuple-element.28), channel_id=1, source_target_pairs={{0,12},{4,0},{8,4},{12,8},{1,13},{5,1},{9,5},{13,9},{2,14},{6,2},{... | collective-permute-start | bytes 202760 | tf_op jit(solution)/shard_map/ppermute | solution.py:279
  11.8 1.5 %collective-permute-start.6 = (bf16[264,128]{1,0:T(8,128)(2,1)S(1)}, bf16[264,128]{1,0:T(8,128)(2,1)S(1)}, u32[]{:S(2)}, u32[]{:S(2)}) collective-permute-start(bf16[264,128]{1,0:T(8,128)(2,1)S(1)} %get-tuple-element.29.refs_0_), channel_id=1, source_target_pairs={{0,2},{2,0},{1,3},{3,1},{4,6},{6,4},{5,7},{7,5},{8,10},{10,8},{9,1... | collective-permute-start | bytes 202760 | tf_op jit(solution)/shard_map/ppermute | solution.py:268
  13.3 0.0 collective-permute-done.4.refs_1_
  13.3 0.8 %collective-permute-start.7 = (bf16[264,128]{1,0:T(8,128)(2,1)S(1)}, bf16[264,128]{1,0:T(8,128)(2,1)S(1)}, u32[]{:S(2)}, u32[]{:S(2)}) collective-permute-start(bf16[264,128]{1,0:T(8,128)(2,1)S(1)} %collective-permute-done.4.refs_1_), channel_id=1, source_target_pairs={{0,2},{2,0},{1,3},{3,1},{4,6},{6,4},{5,7},{7,5},{8,10},{10,8},{9,1... | collective-permute-start | bytes 202760 | tf_op jit(solution)/shard_map/ppermute | solution.py:268
  14.1 1.1 %collective-permute-done.5.refs_2_ = bf16[264,128]{1,0:T(8,128)(2,1)S(1)} collective-permute-done((bf16[264,128]{1,0:T(8,128)(2,1)S(1)}, bf16[264,128]{1,0:T(8,128)(2,1)S(1)}, u32[]{:S(2)}, u32[]{:S(2)}) %collective-permute-start.5) | collective-permute-done | bytes 67616 | tf_op jit(solution)/shard_map/ppermute | solution.py:279
  15.2 1.5 %collective-permute-start.8 = (bf16[264,128]{1,0:T(8,128)(2,1)S(1)}, bf16[264,128]{1,0:T(8,128)(2,1)S(1)}, u32[]{:S(2)}, u32[]{:S(2)}) collective-permute-start(bf16[264,128]{1,0:T(8,128)(2,1)S(1)} %collective-permute-done.5.refs_2_), channel_id=1, source_target_pairs={{0,2},{2,0},{1,3},{3,1},{4,6},{6,4},{5,7},{7,5},{8,10},{10,8},{9,1... | collective-permute-start | bytes 202760 | tf_op jit(solution)/shard_map/ppermute | solution.py:268
  16.7 0.0 collective-permute-done.2.refs_3_
  16.7 0.5 %collective-permute-start.3 = (bf16[264,128]{1,0:T(8,128)(2,1)S(1)}, bf16[264,128]{1,0:T(8,128)(2,1)S(1)}, u32[]{:S(2)}, u32[]{:S(2)}) collective-permute-start(bf16[264,128]{1,0:T(8,128)(2,1)S(1)} %collective-permute-done.2.refs_3_), channel_id=1, source_target_pairs={{0,2},{2,0},{1,3},{3,1},{4,6},{6,4},{5,7},{7,5},{8,10},{10,8},{9,1... | collective-permute-start | bytes 202760 | tf_op jit(solution)/shard_map/ppermute | solution.py:268
  17.3 0.0 collective-permute-done.6.refs_4_
  17.3 0.3 collective-permute-done.7.refs_5_
  17.6 2.5 %collective-permute-done.8.refs_6_ = bf16[264,128]{1,0:T(8,128)(2,1)S(1)} collective-permute-done((bf16[264,128]{1,0:T(8,128)(2,1)S(1)}, bf16[264,128]{1,0:T(8,128)(2,1)S(1)}, u32[]{:S(2)}, u32[]{:S(2)}) %collective-permute-start.8) | collective-permute-done | bytes 67616 | tf_op jit(solution)/shard_map/ppermute | solution.py:268
  20.1 0.4 %combine_first_early.1 = (f32[4,128,256]{2,1,0:T(8,128)S(1)}, f32[8,128]{1,0:T(8,128)S(1)}) custom-call(bf16[264,128]{1,0:T(8,128)(2,1)S(1)} %get-tuple-element.29.refs_0_, bf16[264,128]{1,0:T(8,128)(2,1)S(1)} %collective-permute-done.4.refs_1_, bf16[264,128]{1,0:T(8,128)(2,1)S(1)} %collective-permute-done.5.refs_2_, ...), custom_call_target="tpu_custom_call" | custom-call | tf_op jit(solution)/shard_map/combine_first_early/pallas_call | solution.py:398
  20.5 0.5 %collective-permute-done.3.refs_0_ = bf16[264,128]{1,0:T(8,128)(2,1)S(1)} collective-permute-done((bf16[264,128]{1,0:T(8,128)(2,1)S(1)}, bf16[264,128]{1,0:T(8,128)(2,1)S(1)}, u32[]{:S(2)}, u32[]{:S(2)}) %collective-permute-start.3) | collective-permute-done | bytes 67616 | tf_op jit(solution)/shard_map/ppermute | solution.py:268
  21.0 0.4 combine_first.1
  21.4 0.1 collective-permute-start.9
  21.4 1.5 %collective-permute-done.9.refs_4_ = bf16[528,256]{1,0:T(8,128)(2,1)S(1)} collective-permute-done((bf16[528,256]{1,0:T(8,128)(2,1)S(1)}, bf16[528,256]{1,0:T(8,128)(2,1)S(1)}, u32[]{:S(2)}, u32[]{:S(2)}) %collective-permute-start.9) | collective-permute-done | bytes 270368 | tf_op jit(solution)/shard_map/ppermute | solution.py:427
  23.0 1.6 %products_second.1 = (bf16[264,128]{1,0:T(8,128)(2,1)S(1)}, bf16[264,128]{1,0:T(8,128)(2,1)S(1)}, bf16[264,128]{1,0:T(8,128)(2,1)S(1)}, bf16[264,128]{1,0:T(8,128)(2,1)S(1)}) custom-call(s32[4,128]{1,0:T(4,128)S(1)} %get-tuple-element.23.refs_0_, bf16[8,4,128,256]{3,2,1,0:T(8,128)(2,1)S(1)} %get-tuple-element.24.refs_1_, bf16[8,256,256]{2,1,0:T(8,128)(2,1)S(1)} %copy-done, ...), custom_call_target="tpu_custom_call" | custom-call | flops 1073741824 | bytes 3145728 | tf_op jit(solution)/shard_map/products_second/pallas_call | solution.py:242
  24.6 1.1 %collective-permute-start.12 = (bf16[264,128]{1,0:T(8,128)(2,1)S(1)}, bf16[264,128]{1,0:T(8,128)(2,1)S(1)}, u32[]{:S(2)}, u32[]{:S(2)}) collective-permute-start(bf16[264,128]{1,0:T(8,128)(2,1)S(1)} %get-tuple-element.39), channel_id=1, source_target_pairs={{0,8},{4,12},{8,0},{12,4},{1,9},{5,13},{9,1},{13,5},{2,10},{6,14},... | collective-permute-start | bytes 202760 | tf_op jit(solution)/shard_map/ppermute | solution.py:279
  25.6 2.7 %collective-permute-start.13 = (bf16[264,128]{1,0:T(8,128)(2,1)S(1)}, bf16[264,128]{1,0:T(8,128)(2,1)S(1)}, u32[]{:S(2)}, u32[]{:S(2)}) collective-permute-start(bf16[264,128]{1,0:T(8,128)(2,1)S(1)} %get-tuple-element.40), channel_id=1, source_target_pairs={{0,4},{4,0},{8,12},{12,8},{1,5},{5,1},{9,13},{13,9},{2,6},{6,2},{1... | collective-permute-start | bytes 202760 | tf_op jit(solution)/shard_map/ppermute | solution.py:279
  28.4 0.7 %collective-permute-start.10 = (bf16[264,128]{1,0:T(8,128)(2,1)S(1)}, bf16[264,128]{1,0:T(8,128)(2,1)S(1)}, u32[]{:S(2)}, u32[]{:S(2)}) collective-permute-start(bf16[264,128]{1,0:T(8,128)(2,1)S(1)} %get-tuple-element.37), channel_id=1, source_target_pairs={{0,12},{4,8},{8,4},{12,0},{1,13},{5,9},{9,5},{13,1},{2,14},{6,10},... | collective-permute-start | bytes 202760 | tf_op jit(solution)/shard_map/ppermute | solution.py:279
  29.0 1.1 %collective-permute-start.14 = (bf16[264,128]{1,0:T(8,128)(2,1)S(1)}, bf16[264,128]{1,0:T(8,128)(2,1)S(1)}, u32[]{:S(2)}, u32[]{:S(2)}) collective-permute-start(bf16[264,128]{1,0:T(8,128)(2,1)S(1)} %get-tuple-element.38.refs_0_), channel_id=1, source_target_pairs={{0,2},{2,0},{1,3},{3,1},{4,6},{6,4},{5,7},{7,5},{8,10},{10,8},{9,1... | collective-permute-start | bytes 202760 | tf_op jit(solution)/shard_map/ppermute | solution.py:268
  30.1 1.6 %collective-permute-done.12.refs_1_ = bf16[264,128]{1,0:T(8,128)(2,1)S(1)} collective-permute-done((bf16[264,128]{1,0:T(8,128)(2,1)S(1)}, bf16[264,128]{1,0:T(8,128)(2,1)S(1)}, u32[]{:S(2)}, u32[]{:S(2)}) %collective-permute-start.12) | collective-permute-done | bytes 67616 | tf_op jit(solution)/shard_map/ppermute | solution.py:279
  31.7 0.9 %collective-permute-start.15 = (bf16[264,128]{1,0:T(8,128)(2,1)S(1)}, bf16[264,128]{1,0:T(8,128)(2,1)S(1)}, u32[]{:S(2)}, u32[]{:S(2)}) collective-permute-start(bf16[264,128]{1,0:T(8,128)(2,1)S(1)} %collective-permute-done.12.refs_1_), channel_id=1, source_target_pairs={{0,2},{2,0},{1,3},{3,1},{4,6},{6,4},{5,7},{7,5},{8,10},{10,8},{9,1... | collective-permute-start | bytes 202760 | tf_op jit(solution)/shard_map/ppermute | solution.py:268
  32.6 0.0 collective-permute-done.13.refs_2_
  32.6 1.2 %collective-permute-start.16 = (bf16[264,128]{1,0:T(8,128)(2,1)S(1)}, bf16[264,128]{1,0:T(8,128)(2,1)S(1)}, u32[]{:S(2)}, u32[]{:S(2)}) collective-permute-start(bf16[264,128]{1,0:T(8,128)(2,1)S(1)} %collective-permute-done.13.refs_2_), channel_id=1, source_target_pairs={{0,2},{2,0},{1,3},{3,1},{4,6},{6,4},{5,7},{7,5},{8,10},{10,8},{9,1... | collective-permute-start | bytes 202760 | tf_op jit(solution)/shard_map/ppermute | solution.py:268
  33.8 0.7 %collective-permute-done.10.refs_3_ = bf16[264,128]{1,0:T(8,128)(2,1)S(1)} collective-permute-done((bf16[264,128]{1,0:T(8,128)(2,1)S(1)}, bf16[264,128]{1,0:T(8,128)(2,1)S(1)}, u32[]{:S(2)}, u32[]{:S(2)}) %collective-permute-start.10) | collective-permute-done | bytes 67616 | tf_op jit(solution)/shard_map/ppermute | solution.py:279
  34.4 0.7 %collective-permute-start.11 = (bf16[264,128]{1,0:T(8,128)(2,1)S(1)}, bf16[264,128]{1,0:T(8,128)(2,1)S(1)}, u32[]{:S(2)}, u32[]{:S(2)}) collective-permute-start(bf16[264,128]{1,0:T(8,128)(2,1)S(1)} %collective-permute-done.10.refs_3_), channel_id=1, source_target_pairs={{0,2},{2,0},{1,3},{3,1},{4,6},{6,4},{5,7},{7,5},{8,10},{10,8},{9,1... | collective-permute-start | bytes 202760 | tf_op jit(solution)/shard_map/ppermute | solution.py:268
  35.2 0.7 %copy.9 = bf16[4,128,256]{2,1,0:T(8,128)(2,1)} copy(bf16[4,128,256]{2,1,0:T(8,128)(2,1)S(1)} %get-tuple-element.44) | data formatting | bytes 524288
  35.9 0.0 collective-permute-done.14.refs_4_
  35.9 0.6 %collective-permute-done.15.refs_5_ = bf16[264,128]{1,0:T(8,128)(2,1)S(1)} collective-permute-done((bf16[264,128]{1,0:T(8,128)(2,1)S(1)}, bf16[264,128]{1,0:T(8,128)(2,1)S(1)}, u32[]{:S(2)}, u32[]{:S(2)}) %collective-permute-start.15) | collective-permute-done | bytes 67616 | tf_op jit(solution)/shard_map/ppermute | solution.py:268
  36.5 1.0 %collective-permute-done.16.refs_6_ = bf16[264,128]{1,0:T(8,128)(2,1)S(1)} collective-permute-done((bf16[264,128]{1,0:T(8,128)(2,1)S(1)}, bf16[264,128]{1,0:T(8,128)(2,1)S(1)}, u32[]{:S(2)}, u32[]{:S(2)}) %collective-permute-start.16) | collective-permute-done | bytes 67616 | tf_op jit(solution)/shard_map/ppermute | solution.py:268
  37.5 0.5 %combine_second_early.1 = (f32[4,128,256]{2,1,0:T(8,128)S(1)}, f32[8,128]{1,0:T(8,128)S(1)}) custom-call(bf16[264,128]{1,0:T(8,128)(2,1)S(1)} %get-tuple-element.38.refs_0_, bf16[264,128]{1,0:T(8,128)(2,1)S(1)} %collective-permute-done.12.refs_1_, bf16[264,128]{1,0:T(8,128)(2,1)S(1)} %collective-permute-done.13.refs_2_, ...), custom_call_target="tpu_custom_call" | custom-call | tf_op jit(solution)/shard_map/combine_second_early/pallas_call | solution.py:398
  38.0 0.7 %collective-permute-done.11.refs_0_ = bf16[264,128]{1,0:T(8,128)(2,1)S(1)} collective-permute-done((bf16[264,128]{1,0:T(8,128)(2,1)S(1)}, bf16[264,128]{1,0:T(8,128)(2,1)S(1)}, u32[]{:S(2)}, u32[]{:S(2)}) %collective-permute-start.11) | collective-permute-done | bytes 67616 | tf_op jit(solution)/shard_map/ppermute | solution.py:268
  38.7 0.8 %combine_second.1 = bf16[4,128,256]{2,1,0:T(8,128)(2,1)} custom-call(bf16[264,128]{1,0:T(8,128)(2,1)S(1)} %collective-permute-done.11.refs_0_, s32[8,128]{1,0:T(8,128)S(1)} %get-tuple-element.26.refs_4_.refs_1_, f32[4,128,256]{2,1,0:T(8,128)S(1)} %get-tuple-element.42.refs_2_, f32[8,128]{1,0:T(8,128)S(1)} %get-tuple-element.43.refs_3_), custom_call_target="tpu_custom_call" | custom-call | tf_op jit(solution)/shard_map/combine_second/pallas_call | solution.py:398
Async XLA Ops:
  0.6 2.5 %copy-start = (bf16[8,256,256]{2,1,0:T(8,128)(2,1)S(1)}, bf16[8,256,256]{2,1,0:T(8,128)(2,1)}, u32[]{:S(2)}) copy-start(bf16[8,256,256]{2,1,0:T(8,128)(2,1)} %refs_2_.3) | copy-start | bytes 3145732
  0.6 2.5 %collective-permute-start = (bf16[4,128,256]{2,1,0:T(8,128)(2,1)}, bf16[4,128,256]{2,1,0:T(8,128)(2,1)S(1)}, u32[]{:S(2)}, u32[]{:S(2)}) collective-permute-start(bf16[4,128,256]{2,1,0:T(8,128)(2,1)} %psi_hbm.1), channel_id=1, source_target_pairs={{1,0},{0,1},{3,2},{2,3},{5,4},{4,5},{7,6},{6,7},{9,8},{8,9},{11,10... | collective-permute-start | bytes 786440 | tf_op jit(solution)/shard_map/ppermute | solution.py:427
  1.2 1.9 %collective-permute-start.1 = (f32[4,128]{1,0:T(4,128)}, f32[4,128]{1,0:T(4,128)S(1)}, u32[]{:S(2)}, u32[]{:S(2)}) collective-permute-start(f32[4,128]{1,0:T(4,128)} %energy_hbm.1), channel_id=1, source_target_pairs={{1,0},{0,1},{3,2},{2,3},{5,4},{4,5},{7,6},{6,7},{9,8},{8,9},{11,10... | collective-permute-start | bytes 6152 | tf_op jit(solution)/shard_map/ppermute | solution.py:427
  4.8 8.5 %collective-permute-start.4 = (bf16[264,128]{1,0:T(8,128)(2,1)S(1)}, bf16[264,128]{1,0:T(8,128)(2,1)S(1)}, u32[]{:S(2)}, u32[]{:S(2)}) collective-permute-start(bf16[264,128]{1,0:T(8,128)(2,1)S(1)} %get-tuple-element.30), channel_id=1, source_target_pairs={{0,4},{4,8},{8,12},{12,0},{1,5},{5,9},{9,13},{13,1},{2,6},{6,10},{... | collective-permute-start | bytes 202760 | tf_op jit(solution)/shard_map/ppermute | solution.py:279
  7.8 7.4 %collective-permute-start.5 = (bf16[264,128]{1,0:T(8,128)(2,1)S(1)}, bf16[264,128]{1,0:T(8,128)(2,1)S(1)}, u32[]{:S(2)}, u32[]{:S(2)}) collective-permute-start(bf16[264,128]{1,0:T(8,128)(2,1)S(1)} %get-tuple-element.31), channel_id=1, source_target_pairs={{0,8},{4,12},{8,0},{12,4},{1,9},{5,13},{9,1},{13,5},{2,10},{6,14},... | collective-permute-start | bytes 202760 | tf_op jit(solution)/shard_map/ppermute | solution.py:279
  10.4 6.3 %collective-permute-start.2 = (bf16[264,128]{1,0:T(8,128)(2,1)S(1)}, bf16[264,128]{1,0:T(8,128)(2,1)S(1)}, u32[]{:S(2)}, u32[]{:S(2)}) collective-permute-start(bf16[264,128]{1,0:T(8,128)(2,1)S(1)} %get-tuple-element.28), channel_id=1, source_target_pairs={{0,12},{4,0},{8,4},{12,8},{1,13},{5,1},{9,5},{13,9},{2,14},{6,2},{... | collective-permute-start | bytes 202760 | tf_op jit(solution)/shard_map/ppermute | solution.py:279
  11.8 5.5 %collective-permute-start.6 = (bf16[264,128]{1,0:T(8,128)(2,1)S(1)}, bf16[264,128]{1,0:T(8,128)(2,1)S(1)}, u32[]{:S(2)}, u32[]{:S(2)}) collective-permute-start(bf16[264,128]{1,0:T(8,128)(2,1)S(1)} %get-tuple-element.29.refs_0_), channel_id=1, source_target_pairs={{0,2},{2,0},{1,3},{3,1},{4,6},{6,4},{5,7},{7,5},{8,10},{10,8},{9,1... | collective-permute-start | bytes 202760 | tf_op jit(solution)/shard_map/ppermute | solution.py:268
  13.3 4.3 %collective-permute-start.7 = (bf16[264,128]{1,0:T(8,128)(2,1)S(1)}, bf16[264,128]{1,0:T(8,128)(2,1)S(1)}, u32[]{:S(2)}, u32[]{:S(2)}) collective-permute-start(bf16[264,128]{1,0:T(8,128)(2,1)S(1)} %collective-permute-done.4.refs_1_), channel_id=1, source_target_pairs={{0,2},{2,0},{1,3},{3,1},{4,6},{6,4},{5,7},{7,5},{8,10},{10,8},{9,1... | collective-permute-start | bytes 202760 | tf_op jit(solution)/shard_map/ppermute | solution.py:268
  15.2 4.8 %collective-permute-start.8 = (bf16[264,128]{1,0:T(8,128)(2,1)S(1)}, bf16[264,128]{1,0:T(8,128)(2,1)S(1)}, u32[]{:S(2)}, u32[]{:S(2)}) collective-permute-start(bf16[264,128]{1,0:T(8,128)(2,1)S(1)} %collective-permute-done.5.refs_2_), channel_id=1, source_target_pairs={{0,2},{2,0},{1,3},{3,1},{4,6},{6,4},{5,7},{7,5},{8,10},{10,8},{9,1... | collective-permute-start | bytes 202760 | tf_op jit(solution)/shard_map/ppermute | solution.py:268
  16.7 4.3 %collective-permute-start.3 = (bf16[264,128]{1,0:T(8,128)(2,1)S(1)}, bf16[264,128]{1,0:T(8,128)(2,1)S(1)}, u32[]{:S(2)}, u32[]{:S(2)}) collective-permute-start(bf16[264,128]{1,0:T(8,128)(2,1)S(1)} %collective-permute-done.2.refs_3_), channel_id=1, source_target_pairs={{0,2},{2,0},{1,3},{3,1},{4,6},{6,4},{5,7},{7,5},{8,10},{10,8},{9,1... | collective-permute-start | bytes 202760 | tf_op jit(solution)/shard_map/ppermute | solution.py:268
  21.4 1.6 %collective-permute-start.9 = (bf16[528,256]{1,0:T(8,128)(2,1)S(1)}, bf16[528,256]{1,0:T(8,128)(2,1)S(1)}, u32[]{:S(2)}, u32[]{:S(2)}) collective-permute-start(bf16[528,256]{1,0:T(8,128)(2,1)S(1)} %get-tuple-element.36.refs_3_.refs_7_), channel_id=1, source_target_pairs={{1,0},{0,1},{3,2},{2,3},{5,4},{4,5},{7,6},{6,7},{9,8},{8,9},{11,10... | collective-permute-start | bytes 811016 | tf_op jit(solution)/shard_map/ppermute | solution.py:427
  24.6 7.2 %collective-permute-start.12 = (bf16[264,128]{1,0:T(8,128)(2,1)S(1)}, bf16[264,128]{1,0:T(8,128)(2,1)S(1)}, u32[]{:S(2)}, u32[]{:S(2)}) collective-permute-start(bf16[264,128]{1,0:T(8,128)(2,1)S(1)} %get-tuple-element.39), channel_id=1, source_target_pairs={{0,8},{4,12},{8,0},{12,4},{1,9},{5,13},{9,1},{13,5},{2,10},{6,14},... | collective-permute-start | bytes 202760 | tf_op jit(solution)/shard_map/ppermute | solution.py:279
  25.6 7.0 %collective-permute-start.13 = (bf16[264,128]{1,0:T(8,128)(2,1)S(1)}, bf16[264,128]{1,0:T(8,128)(2,1)S(1)}, u32[]{:S(2)}, u32[]{:S(2)}) collective-permute-start(bf16[264,128]{1,0:T(8,128)(2,1)S(1)} %get-tuple-element.40), channel_id=1, source_target_pairs={{0,4},{4,0},{8,12},{12,8},{1,5},{5,1},{9,13},{13,9},{2,6},{6,2},{1... | collective-permute-start | bytes 202760 | tf_op jit(solution)/shard_map/ppermute | solution.py:279
  28.4 6.1 %collective-permute-start.10 = (bf16[264,128]{1,0:T(8,128)(2,1)S(1)}, bf16[264,128]{1,0:T(8,128)(2,1)S(1)}, u32[]{:S(2)}, u32[]{:S(2)}) collective-permute-start(bf16[264,128]{1,0:T(8,128)(2,1)S(1)} %get-tuple-element.37), channel_id=1, source_target_pairs={{0,12},{4,8},{8,4},{12,0},{1,13},{5,9},{9,5},{13,1},{2,14},{6,10},... | collective-permute-start | bytes 202760 | tf_op jit(solution)/shard_map/ppermute | solution.py:279
  29.0 6.8 %collective-permute-start.14 = (bf16[264,128]{1,0:T(8,128)(2,1)S(1)}, bf16[264,128]{1,0:T(8,128)(2,1)S(1)}, u32[]{:S(2)}, u32[]{:S(2)}) collective-permute-start(bf16[264,128]{1,0:T(8,128)(2,1)S(1)} %get-tuple-element.38.refs_0_), channel_id=1, source_target_pairs={{0,2},{2,0},{1,3},{3,1},{4,6},{6,4},{5,7},{7,5},{8,10},{10,8},{9,1... | collective-permute-start | bytes 202760 | tf_op jit(solution)/shard_map/ppermute | solution.py:268
  31.7 4.7 %collective-permute-start.15 = (bf16[264,128]{1,0:T(8,128)(2,1)S(1)}, bf16[264,128]{1,0:T(8,128)(2,1)S(1)}, u32[]{:S(2)}, u32[]{:S(2)}) collective-permute-start(bf16[264,128]{1,0:T(8,128)(2,1)S(1)} %collective-permute-done.12.refs_1_), channel_id=1, source_target_pairs={{0,2},{2,0},{1,3},{3,1},{4,6},{6,4},{5,7},{7,5},{8,10},{10,8},{9,1... | collective-permute-start | bytes 202760 | tf_op jit(solution)/shard_map/ppermute | solution.py:268
  32.6 4.9 %collective-permute-start.16 = (bf16[264,128]{1,0:T(8,128)(2,1)S(1)}, bf16[264,128]{1,0:T(8,128)(2,1)S(1)}, u32[]{:S(2)}, u32[]{:S(2)}) collective-permute-start(bf16[264,128]{1,0:T(8,128)(2,1)S(1)} %collective-permute-done.13.refs_2_), channel_id=1, source_target_pairs={{0,2},{2,0},{1,3},{3,1},{4,6},{6,4},{5,7},{7,5},{8,10},{10,8},{9,1... | collective-permute-start | bytes 202760 | tf_op jit(solution)/shard_map/ppermute | solution.py:268
  34.4 4.3 %collective-permute-start.11 = (bf16[264,128]{1,0:T(8,128)(2,1)S(1)}, bf16[264,128]{1,0:T(8,128)(2,1)S(1)}, u32[]{:S(2)}, u32[]{:S(2)}) collective-permute-start(bf16[264,128]{1,0:T(8,128)(2,1)S(1)} %collective-permute-done.10.refs_3_), channel_id=1, source_target_pairs={{0,2},{2,0},{1,3},{3,1},{4,6},{6,4},{5,7},{7,5},{8,10},{10,8},{9,1... | collective-permute-start | bytes 202760 | tf_op jit(solution)/shard_map/ppermute | solution.py:268

commit v3 on v1

--- a/solution.py
+++ b/solution.py
@@ -408,7 +408,7 @@
     split = sec_count * op_count <= 8
     can_pair = sec_count & (sec_count - 1) == 0
     steps = list(range(1, sec_count))
-    first_plan = (False, steps, sec_count - 1)
+    first_plan = (can_pair, steps[1:2] + steps[:1] + steps[2:], sec_count - 1)
     second_plan = (can_pair, steps[1:2] + steps[:1] + steps[2:], sec_count - 1)
     params = pltpu.CompilerParams(vmem_limit_bytes=VMEM_BYTES)
     vec_shape = (sec_dev, half, width)

time: 39.6 us -> 39.5 us (level)
  waiting for transfers between devices: 10.6 us -> 9.85 us
  starting transfers between devices: 20.3 us -> 21 us
    ppermute x8, starting transfers between devices: 8.25 us -> 10.3 us  [exchange(): lax.ppermute(packet, 'op', turn)]
    ppermute x6, starting transfers between devices: 11.4 us -> 10.1 us  [exchange(): arrived[step] = lax.ppermute(packets[step], 'sec', turn)]
    ppermute x8, waiting for transfers between devices: 5.67 us -> 4.45 us  [exchange(): lax.ppermute(packet, 'op', turn)]
    ppermute x6, waiting for transfers between devices: 3.39 us -> 3.87 us  [exchange(): arrived[step] = lax.ppermute(packets[step], 'sec', turn)]
  transfers between devices with their start and end apart: 17 -> 17, of which waited for: 10 -> 9; matrix products, arithmetic and copies ran while one was open for 2% -> 2% of each run, Pallas kernels for 7% -> 7%
where the time goes in v3:
time: 39.5 us; the launch traced here: 39.4 us
  starting transfers between devices  21 us (53%)
  waiting for transfers between devices  9.85 us (25%)
  Pallas kernels  7.07 us (18%)
  between operations  0.72 us (2%)
  local copies, waits for them, and re-layouts  0.71 us (2%)
    ppermute x8, starting transfers between devices, exchange(): lax.ppermute(packet, 'op', turn)  10.3 us
    ppermute x6, starting transfers between devices, exchange(): arrived[step] = lax.ppermute(packets[step], 'sec', turn)  10.1 us
    ppermute x8, waiting for transfers between devices, exchange(): lax.ppermute(packet, 'op', turn)  4.45 us
    ppermute x6, waiting for transfers between devices, exchange(): arrived[step] = lax.ppermute(packets[step], 'sec', turn)  3.87 us
    pallas_call x2, Pallas kernels, sigma_packets(): pl.pallas_call(functools.partial(product_kernel, is_first, split, paired,...  3.11 us
    pallas_call x4, Pallas kernels, call(): pl.pallas_call(kernel, out_shape=outs, in_specs=[whole(pltpu.VMEM)] * len...  2.11 us
    pallas_call x1, Pallas kernels, body(): pl.pallas_call(load_kernel, out_shape=[vec_bf16, jax.ShapeDtypeStruct(lef...  1.84 us
    ppermute x3, waiting for transfers between devices, from_others(): arrays.append(lax.ppermute(array, 'rep', turn))  1.54 us
  transfers between devices with their start and end apart: 17, of which 9 were waited for; matrix products, arithmetic and copies ran while one was open for 2% of the time, Pallas kernels for 7%

profile of v3, /device:TPU:0, one launch (start us, length us, event | category | flops | bytes accessed | tf_op | source)
XLA Modules:
  0.0 39.4 jit_solution(6268481243310042181)
XLA Ops:
  0.6 0.0 copy-start
  0.6 0.5 %collective-permute-start = (bf16[4,128,256]{2,1,0:T(8,128)(2,1)}, bf16[4,128,256]{2,1,0:T(8,128)(2,1)S(1)}, u32[]{:S(2)}, u32[]{:S(2)}) collective-permute-start(bf16[4,128,256]{2,1,0:T(8,128)(2,1)} %psi_hbm.1), channel_id=1, source_target_pairs={{1,0},{0,1},{3,2},{2,3},{5,4},{4,5},{7,6},{6,7},{9,8},{8,9},{11,10... | collective-permute-start | bytes 786440 | tf_op jit(solution)/shard_map/ppermute | solution.py:421
  1.2 0.1 collective-permute-start.1
  1.2 1.8 %load.1 = (bf16[4,128,256]{2,1,0:T(8,128)(2,1)S(1)}, bf16[8,4,128,256]{3,2,1,0:T(8,128)(2,1)S(1)}, s32[4,128]{1,0:T(4,128)S(1)}, s32[8,128]{1,0:T(8,128)S(1)}, f...) custom-call(bf16[4,128,256]{2,1,0:T(8,128)(2,1)} %psi_hbm.1, bf16[8,4,128,256]{3,2,1,0:T(8,128)(2,1)} %left_hbm.1, ...), custom_call_target="tpu_custom_call" | custom-call | tf_op jit(solution)/shard_map/load/pallas_call | solution.py:426
  3.1 0.0 collective-permute-done.1.refs_7_
  3.1 0.0 collective-permute-done.refs_6_
  3.1 0.0 copy-done
  3.1 1.6 %products_first.1 = (bf16[264,128]{1,0:T(8,128)(2,1)S(1)}, bf16[264,128]{1,0:T(8,128)(2,1)S(1)}, bf16[264,128]{1,0:T(8,128)(2,1)S(1)}, bf16[264,128]{1,0:T(8,128)(2,1)S(1)}) custom-call(s32[4,128]{1,0:T(4,128)S(1)} %get-tuple-element.23.refs_0_, bf16[8,4,128,256]{3,2,1,0:T(8,128)(2,1)S(1)} %get-tuple-element.24.refs_1_, bf16[8,256,256]{2,1,0:T(8,128)(2,1)S(1)} %copy-done, ...), custom_call_target="tpu_custom_call" | custom-call | flops 1073741824 | bytes 3145728 | tf_op jit(solution)/shard_map/products_first/pallas_call | solution.py:236
  4.7 4.1 %collective-permute-start.4 = (bf16[264,128]{1,0:T(8,128)(2,1)S(1)}, bf16[264,128]{1,0:T(8,128)(2,1)S(1)}, u32[]{:S(2)}, u32[]{:S(2)}) collective-permute-start(bf16[264,128]{1,0:T(8,128)(2,1)S(1)} %get-tuple-element.30), channel_id=1, source_target_pairs={{0,8},{4,12},{8,0},{12,4},{1,9},{5,13},{9,1},{13,5},{2,10},{6,14},... | collective-permute-start | bytes 202760 | tf_op jit(solution)/shard_map/ppermute | solution.py:273
  8.8 1.6 %collective-permute-start.5 = (bf16[264,128]{1,0:T(8,128)(2,1)S(1)}, bf16[264,128]{1,0:T(8,128)(2,1)S(1)}, u32[]{:S(2)}, u32[]{:S(2)}) collective-permute-start(bf16[264,128]{1,0:T(8,128)(2,1)S(1)} %get-tuple-element.31), channel_id=1, source_target_pairs={{0,4},{4,0},{8,12},{12,8},{1,5},{5,1},{9,13},{13,9},{2,6},{6,2},{1... | collective-permute-start | bytes 202760 | tf_op jit(solution)/shard_map/ppermute | solution.py:273
  10.4 0.0 collective-permute-start.2
  10.4 1.7 %collective-permute-start.6 = (bf16[264,128]{1,0:T(8,128)(2,1)S(1)}, bf16[264,128]{1,0:T(8,128)(2,1)S(1)}, u32[]{:S(2)}, u32[]{:S(2)}) collective-permute-start(bf16[264,128]{1,0:T(8,128)(2,1)S(1)} %get-tuple-element.29.refs_0_), channel_id=1, source_target_pairs={{0,2},{2,0},{1,3},{3,1},{4,6},{6,4},{5,7},{7,5},{8,10},{10,8},{9,1... | collective-permute-start | bytes 202760 | tf_op jit(solution)/shard_map/ppermute | solution.py:262
  12.1 0.0 collective-permute-done.4.refs_1_
  12.1 2.0 %collective-permute-start.7 = (bf16[264,128]{1,0:T(8,128)(2,1)S(1)}, bf16[264,128]{1,0:T(8,128)(2,1)S(1)}, u32[]{:S(2)}, u32[]{:S(2)}) collective-permute-start(bf16[264,128]{1,0:T(8,128)(2,1)S(1)} %collective-permute-done.4.refs_1_), channel_id=1, source_target_pairs={{0,2},{2,0},{1,3},{3,1},{4,6},{6,4},{5,7},{7,5},{8,10},{10,8},{9,1... | collective-permute-start | bytes 202760 | tf_op jit(solution)/shard_map/ppermute | solution.py:262
  14.1 0.0 collective-permute-done.5.refs_2_
  14.1 0.6 %collective-permute-start.8 = (bf16[264,128]{1,0:T(8,128)(2,1)S(1)}, bf16[264,128]{1,0:T(8,128)(2,1)S(1)}, u32[]{:S(2)}, u32[]{:S(2)}) collective-permute-start(bf16[264,128]{1,0:T(8,128)(2,1)S(1)} %collective-permute-done.5.refs_2_), channel_id=1, source_target_pairs={{0,2},{2,0},{1,3},{3,1},{4,6},{6,4},{5,7},{7,5},{8,10},{10,8},{9,1... | collective-permute-start | bytes 202760 | tf_op jit(solution)/shard_map/ppermute | solution.py:262
  14.7 1.8 %collective-permute-done.2.refs_3_ = bf16[264,128]{1,0:T(8,128)(2,1)S(1)} collective-permute-done((bf16[264,128]{1,0:T(8,128)(2,1)S(1)}, bf16[264,128]{1,0:T(8,128)(2,1)S(1)}, u32[]{:S(2)}, u32[]{:S(2)}) %collective-permute-start.2) | collective-permute-done | bytes 67616 | tf_op jit(solution)/shard_map/ppermute | solution.py:273
  16.4 1.5 %collective-permute-start.3 = (bf16[264,128]{1,0:T(8,128)(2,1)S(1)}, bf16[264,128]{1,0:T(8,128)(2,1)S(1)}, u32[]{:S(2)}, u32[]{:S(2)}) collective-permute-start(bf16[264,128]{1,0:T(8,128)(2,1)S(1)} %collective-permute-done.2.refs_3_), channel_id=1, source_target_pairs={{0,2},{2,0},{1,3},{3,1},{4,6},{6,4},{5,7},{7,5},{8,10},{10,8},{9,1... | collective-permute-start | bytes 202760 | tf_op jit(solution)/shard_map/ppermute | solution.py:262
  17.9 0.0 collective-permute-done.6.refs_4_
  17.9 0.0 collective-permute-done.7.refs_5_
  17.9 1.0 %collective-permute-done.8.refs_6_ = bf16[264,128]{1,0:T(8,128)(2,1)S(1)} collective-permute-done((bf16[264,128]{1,0:T(8,128)(2,1)S(1)}, bf16[264,128]{1,0:T(8,128)(2,1)S(1)}, u32[]{:S(2)}, u32[]{:S(2)}) %collective-permute-start.8) | collective-permute-done | bytes 67616 | tf_op jit(solution)/shard_map/ppermute | solution.py:262
  19.0 0.4 %combine_first_early.1 = (f32[4,128,256]{2,1,0:T(8,128)S(1)}, f32[8,128]{1,0:T(8,128)S(1)}) custom-call(bf16[264,128]{1,0:T(8,128)(2,1)S(1)} %get-tuple-element.29.refs_0_, bf16[264,128]{1,0:T(8,128)(2,1)S(1)} %collective-permute-done.4.refs_1_, bf16[264,128]{1,0:T(8,128)(2,1)S(1)} %collective-permute-done.5.refs_2_, ...), custom_call_target="tpu_custom_call" | custom-call | tf_op jit(solution)/shard_map/combine_first_early/pallas_call | solution.py:392
  19.4 1.3 %collective-permute-done.3.refs_0_ = bf16[264,128]{1,0:T(8,128)(2,1)S(1)} collective-permute-done((bf16[264,128]{1,0:T(8,128)(2,1)S(1)}, bf16[264,128]{1,0:T(8,128)(2,1)S(1)}, u32[]{:S(2)}, u32[]{:S(2)}) %collective-permute-start.3) | collective-permute-done | bytes 67616 | tf_op jit(solution)/shard_map/ppermute | solution.py:262
  20.7 0.4 combine_first.1
  21.1 0.1 collective-permute-start.9
  21.2 1.5 %collective-permute-done.9.refs_4_ = bf16[528,256]{1,0:T(8,128)(2,1)S(1)} collective-permute-done((bf16[528,256]{1,0:T(8,128)(2,1)S(1)}, bf16[528,256]{1,0:T(8,128)(2,1)S(1)}, u32[]{:S(2)}, u32[]{:S(2)}) %collective-permute-start.9) | collective-permute-done | bytes 270368 | tf_op jit(solution)/shard_map/ppermute | solution.py:421
  22.7 1.5 %products_second.1 = (bf16[264,128]{1,0:T(8,128)(2,1)S(1)}, bf16[264,128]{1,0:T(8,128)(2,1)S(1)}, bf16[264,128]{1,0:T(8,128)(2,1)S(1)}, bf16[264,128]{1,0:T(8,128)(2,1)S(1)}) custom-call(s32[4,128]{1,0:T(4,128)S(1)} %get-tuple-element.23.refs_0_, bf16[8,4,128,256]{3,2,1,0:T(8,128)(2,1)S(1)} %get-tuple-element.24.refs_1_, bf16[8,256,256]{2,1,0:T(8,128)(2,1)S(1)} %copy-done, ...), custom_call_target="tpu_custom_call" | custom-call | flops 1073741824 | bytes 3145728 | tf_op jit(solution)/shard_map/products_second/pallas_call | solution.py:236
  24.2 1.8 %collective-permute-start.12 = (bf16[264,128]{1,0:T(8,128)(2,1)S(1)}, bf16[264,128]{1,0:T(8,128)(2,1)S(1)}, u32[]{:S(2)}, u32[]{:S(2)}) collective-permute-start(bf16[264,128]{1,0:T(8,128)(2,1)S(1)} %get-tuple-element.39), channel_id=1, source_target_pairs={{0,8},{4,12},{8,0},{12,4},{1,9},{5,13},{9,1},{13,5},{2,10},{6,14},... | collective-permute-start | bytes 202760 | tf_op jit(solution)/shard_map/ppermute | solution.py:273
  26.0 2.2 %collective-permute-start.13 = (bf16[264,128]{1,0:T(8,128)(2,1)S(1)}, bf16[264,128]{1,0:T(8,128)(2,1)S(1)}, u32[]{:S(2)}, u32[]{:S(2)}) collective-permute-start(bf16[264,128]{1,0:T(8,128)(2,1)S(1)} %get-tuple-element.40), channel_id=1, source_target_pairs={{0,4},{4,0},{8,12},{12,8},{1,5},{5,1},{9,13},{13,9},{2,6},{6,2},{1... | collective-permute-start | bytes 202760 | tf_op jit(solution)/shard_map/ppermute | solution.py:273
  28.2 0.5 %collective-permute-start.10 = (bf16[264,128]{1,0:T(8,128)(2,1)S(1)}, bf16[264,128]{1,0:T(8,128)(2,1)S(1)}, u32[]{:S(2)}, u32[]{:S(2)}) collective-permute-start(bf16[264,128]{1,0:T(8,128)(2,1)S(1)} %get-tuple-element.37), channel_id=1, source_target_pairs={{0,12},{4,8},{8,4},{12,0},{1,13},{5,9},{9,5},{13,1},{2,14},{6,10},... | collective-permute-start | bytes 202760 | tf_op jit(solution)/shard_map/ppermute | solution.py:273
  28.7 1.5 %collective-permute-start.14 = (bf16[264,128]{1,0:T(8,128)(2,1)S(1)}, bf16[264,128]{1,0:T(8,128)(2,1)S(1)}, u32[]{:S(2)}, u32[]{:S(2)}) collective-permute-start(bf16[264,128]{1,0:T(8,128)(2,1)S(1)} %get-tuple-element.38.refs_0_), channel_id=1, source_target_pairs={{0,2},{2,0},{1,3},{3,1},{4,6},{6,4},{5,7},{7,5},{8,10},{10,8},{9,1... | collective-permute-start | bytes 202760 | tf_op jit(solution)/shard_map/ppermute | solution.py:262
  30.2 1.2 %collective-permute-done.12.refs_1_ = bf16[264,128]{1,0:T(8,128)(2,1)S(1)} collective-permute-done((bf16[264,128]{1,0:T(8,128)(2,1)S(1)}, bf16[264,128]{1,0:T(8,128)(2,1)S(1)}, u32[]{:S(2)}, u32[]{:S(2)}) %collective-permute-start.12) | collective-permute-done | bytes 67616 | tf_op jit(solution)/shard_map/ppermute | solution.py:273
  31.3 1.2 %collective-permute-start.15 = (bf16[264,128]{1,0:T(8,128)(2,1)S(1)}, bf16[264,128]{1,0:T(8,128)(2,1)S(1)}, u32[]{:S(2)}, u32[]{:S(2)}) collective-permute-start(bf16[264,128]{1,0:T(8,128)(2,1)S(1)} %collective-permute-done.12.refs_1_), channel_id=1, source_target_pairs={{0,2},{2,0},{1,3},{3,1},{4,6},{6,4},{5,7},{7,5},{8,10},{10,8},{9,1... | collective-permute-start | bytes 202760 | tf_op jit(solution)/shard_map/ppermute | solution.py:262
  32.6 0.0 collective-permute-done.13.refs_2_
  32.6 0.8 %collective-permute-start.16 = (bf16[264,128]{1,0:T(8,128)(2,1)S(1)}, bf16[264,128]{1,0:T(8,128)(2,1)S(1)}, u32[]{:S(2)}, u32[]{:S(2)}) collective-permute-start(bf16[264,128]{1,0:T(8,128)(2,1)S(1)} %collective-permute-done.13.refs_2_), channel_id=1, source_target_pairs={{0,2},{2,0},{1,3},{3,1},{4,6},{6,4},{5,7},{7,5},{8,10},{10,8},{9,1... | collective-permute-start | bytes 202760 | tf_op jit(solution)/shard_map/ppermute | solution.py:262
  33.4 0.9 %collective-permute-done.10.refs_3_ = bf16[264,128]{1,0:T(8,128)(2,1)S(1)} collective-permute-done((bf16[264,128]{1,0:T(8,128)(2,1)S(1)}, bf16[264,128]{1,0:T(8,128)(2,1)S(1)}, u32[]{:S(2)}, u32[]{:S(2)}) %collective-permute-start.10) | collective-permute-done | bytes 67616 | tf_op jit(solution)/shard_map/ppermute | solution.py:273
  34.2 1.0 %collective-permute-start.11 = (bf16[264,128]{1,0:T(8,128)(2,1)S(1)}, bf16[264,128]{1,0:T(8,128)(2,1)S(1)}, u32[]{:S(2)}, u32[]{:S(2)}) collective-permute-start(bf16[264,128]{1,0:T(8,128)(2,1)S(1)} %collective-permute-done.10.refs_3_), channel_id=1, source_target_pairs={{0,2},{2,0},{1,3},{3,1},{4,6},{6,4},{5,7},{7,5},{8,10},{10,8},{9,1... | collective-permute-start | bytes 202760 | tf_op jit(solution)/shard_map/ppermute | solution.py:262
  35.2 0.7 %copy.9 = bf16[4,128,256]{2,1,0:T(8,128)(2,1)} copy(bf16[4,128,256]{2,1,0:T(8,128)(2,1)S(1)} %get-tuple-element.44) | data formatting | bytes 524288
  35.9 0.0 collective-permute-done.14.refs_4_
  35.9 0.3 collective-permute-done.15.refs_5_
  36.3 1.1 %collective-permute-done.16.refs_6_ = bf16[264,128]{1,0:T(8,128)(2,1)S(1)} collective-permute-done((bf16[264,128]{1,0:T(8,128)(2,1)S(1)}, bf16[264,128]{1,0:T(8,128)(2,1)S(1)}, u32[]{:S(2)}, u32[]{:S(2)}) %collective-permute-start.16) | collective-permute-done | bytes 67616 | tf_op jit(solution)/shard_map/ppermute | solution.py:262
  37.4 0.5 %combine_second_early.1 = (f32[4,128,256]{2,1,0:T(8,128)S(1)}, f32[8,128]{1,0:T(8,128)S(1)}) custom-call(bf16[264,128]{1,0:T(8,128)(2,1)S(1)} %get-tuple-element.38.refs_0_, bf16[264,128]{1,0:T(8,128)(2,1)S(1)} %collective-permute-done.12.refs_1_, bf16[264,128]{1,0:T(8,128)(2,1)S(1)} %collective-permute-done.13.refs_2_, ...), custom_call_target="tpu_custom_call" | custom-call | tf_op jit(solution)/shard_map/combine_second_early/pallas_call | solution.py:392
  37.9 0.7 %collective-permute-done.11.refs_0_ = bf16[264,128]{1,0:T(8,128)(2,1)S(1)} collective-permute-done((bf16[264,128]{1,0:T(8,128)(2,1)S(1)}, bf16[264,128]{1,0:T(8,128)(2,1)S(1)}, u32[]{:S(2)}, u32[]{:S(2)}) %collective-permute-start.11) | collective-permute-done | bytes 67616 | tf_op jit(solution)/shard_map/ppermute | solution.py:262
  38.5 0.8 %combine_second.1 = bf16[4,128,256]{2,1,0:T(8,128)(2,1)} custom-call(bf16[264,128]{1,0:T(8,128)(2,1)S(1)} %collective-permute-done.11.refs_0_, s32[8,128]{1,0:T(8,128)S(1)} %get-tuple-element.26.refs_4_.refs_1_, f32[4,128,256]{2,1,0:T(8,128)S(1)} %get-tuple-element.42.refs_2_, f32[8,128]{1,0:T(8,128)S(1)} %get-tuple-element.43.refs_3_), custom_call_target="tpu_custom_call" | custom-call | tf_op jit(solution)/shard_map/combine_second/pallas_call | solution.py:392
Async XLA Ops:
  0.6 2.5 %copy-start = (bf16[8,256,256]{2,1,0:T(8,128)(2,1)S(1)}, bf16[8,256,256]{2,1,0:T(8,128)(2,1)}, u32[]{:S(2)}) copy-start(bf16[8,256,256]{2,1,0:T(8,128)(2,1)} %refs_2_.3) | copy-start | bytes 3145732
  0.6 2.5 %collective-permute-start = (bf16[4,128,256]{2,1,0:T(8,128)(2,1)}, bf16[4,128,256]{2,1,0:T(8,128)(2,1)S(1)}, u32[]{:S(2)}, u32[]{:S(2)}) collective-permute-start(bf16[4,128,256]{2,1,0:T(8,128)(2,1)} %psi_hbm.1), channel_id=1, source_target_pairs={{1,0},{0,1},{3,2},{2,3},{5,4},{4,5},{7,6},{6,7},{9,8},{8,9},{11,10... | collective-permute-start | bytes 786440 | tf_op jit(solution)/shard_map/ppermute | solution.py:421
  1.2 1.9 %collective-permute-start.1 = (f32[4,128]{1,0:T(4,128)}, f32[4,128]{1,0:T(4,128)S(1)}, u32[]{:S(2)}, u32[]{:S(2)}) collective-permute-start(f32[4,128]{1,0:T(4,128)} %energy_hbm.1), channel_id=1, source_target_pairs={{1,0},{0,1},{3,2},{2,3},{5,4},{4,5},{7,6},{6,7},{9,8},{8,9},{11,10... | collective-permute-start | bytes 6152 | tf_op jit(solution)/shard_map/ppermute | solution.py:421
  4.7 7.4 %collective-permute-start.4 = (bf16[264,128]{1,0:T(8,128)(2,1)S(1)}, bf16[264,128]{1,0:T(8,128)(2,1)S(1)}, u32[]{:S(2)}, u32[]{:S(2)}) collective-permute-start(bf16[264,128]{1,0:T(8,128)(2,1)S(1)} %get-tuple-element.30), channel_id=1, source_target_pairs={{0,8},{4,12},{8,0},{12,4},{1,9},{5,13},{9,1},{13,5},{2,10},{6,14},... | collective-permute-start | bytes 202760 | tf_op jit(solution)/shard_map/ppermute | solution.py:273
  8.8 5.3 %collective-permute-start.5 = (bf16[264,128]{1,0:T(8,128)(2,1)S(1)}, bf16[264,128]{1,0:T(8,128)(2,1)S(1)}, u32[]{:S(2)}, u32[]{:S(2)}) collective-permute-start(bf16[264,128]{1,0:T(8,128)(2,1)S(1)} %get-tuple-element.31), channel_id=1, source_target_pairs={{0,4},{4,0},{8,12},{12,8},{1,5},{5,1},{9,13},{13,9},{2,6},{6,2},{1... | collective-permute-start | bytes 202760 | tf_op jit(solution)/shard_map/ppermute | solution.py:273
  10.4 6.1 %collective-permute-start.2 = (bf16[264,128]{1,0:T(8,128)(2,1)S(1)}, bf16[264,128]{1,0:T(8,128)(2,1)S(1)}, u32[]{:S(2)}, u32[]{:S(2)}) collective-permute-start(bf16[264,128]{1,0:T(8,128)(2,1)S(1)} %get-tuple-element.28), channel_id=1, source_target_pairs={{0,12},{4,8},{8,4},{12,0},{1,13},{5,9},{9,5},{13,1},{2,14},{6,10},... | collective-permute-start | bytes 202760 | tf_op jit(solution)/shard_map/ppermute | solution.py:273
  10.4 7.6 %collective-permute-start.6 = (bf16[264,128]{1,0:T(8,128)(2,1)S(1)}, bf16[264,128]{1,0:T(8,128)(2,1)S(1)}, u32[]{:S(2)}, u32[]{:S(2)}) collective-permute-start(bf16[264,128]{1,0:T(8,128)(2,1)S(1)} %get-tuple-element.29.refs_0_), channel_id=1, source_target_pairs={{0,2},{2,0},{1,3},{3,1},{4,6},{6,4},{5,7},{7,5},{8,10},{10,8},{9,1... | collective-permute-start | bytes 202760 | tf_op jit(solution)/shard_map/ppermute | solution.py:262
  12.1 5.8 %collective-permute-start.7 = (bf16[264,128]{1,0:T(8,128)(2,1)S(1)}, bf16[264,128]{1,0:T(8,128)(2,1)S(1)}, u32[]{:S(2)}, u32[]{:S(2)}) collective-permute-start(bf16[264,128]{1,0:T(8,128)(2,1)S(1)} %collective-permute-done.4.refs_1_), channel_id=1, source_target_pairs={{0,2},{2,0},{1,3},{3,1},{4,6},{6,4},{5,7},{7,5},{8,10},{10,8},{9,1... | collective-permute-start | bytes 202760 | tf_op jit(solution)/shard_map/ppermute | solution.py:262
  14.1 4.9 %collective-permute-start.8 = (bf16[264,128]{1,0:T(8,128)(2,1)S(1)}, bf16[264,128]{1,0:T(8,128)(2,1)S(1)}, u32[]{:S(2)}, u32[]{:S(2)}) collective-permute-start(bf16[264,128]{1,0:T(8,128)(2,1)S(1)} %collective-permute-done.5.refs_2_), channel_id=1, source_target_pairs={{0,2},{2,0},{1,3},{3,1},{4,6},{6,4},{5,7},{7,5},{8,10},{10,8},{9,1... | collective-permute-start | bytes 202760 | tf_op jit(solution)/shard_map/ppermute | solution.py:262
  16.4 4.3 %collective-permute-start.3 = (bf16[264,128]{1,0:T(8,128)(2,1)S(1)}, bf16[264,128]{1,0:T(8,128)(2,1)S(1)}, u32[]{:S(2)}, u32[]{:S(2)}) collective-permute-start(bf16[264,128]{1,0:T(8,128)(2,1)S(1)} %collective-permute-done.2.refs_3_), channel_id=1, source_target_pairs={{0,2},{2,0},{1,3},{3,1},{4,6},{6,4},{5,7},{7,5},{8,10},{10,8},{9,1... | collective-permute-start | bytes 202760 | tf_op jit(solution)/shard_map/ppermute | solution.py:262
  21.1 1.6 %collective-permute-start.9 = (bf16[528,256]{1,0:T(8,128)(2,1)S(1)}, bf16[528,256]{1,0:T(8,128)(2,1)S(1)}, u32[]{:S(2)}, u32[]{:S(2)}) collective-permute-start(bf16[528,256]{1,0:T(8,128)(2,1)S(1)} %get-tuple-element.36.refs_3_.refs_7_), channel_id=1, source_target_pairs={{1,0},{0,1},{3,2},{2,3},{5,4},{4,5},{7,6},{6,7},{9,8},{8,9},{11,10... | collective-permute-start | bytes 811016 | tf_op jit(solution)/shard_map/ppermute | solution.py:421
  24.2 7.1 %collective-permute-start.12 = (bf16[264,128]{1,0:T(8,128)(2,1)S(1)}, bf16[264,128]{1,0:T(8,128)(2,1)S(1)}, u32[]{:S(2)}, u32[]{:S(2)}) collective-permute-start(bf16[264,128]{1,0:T(8,128)(2,1)S(1)} %get-tuple-element.39), channel_id=1, source_target_pairs={{0,8},{4,12},{8,0},{12,4},{1,9},{5,13},{9,1},{13,5},{2,10},{6,14},... | collective-permute-start | bytes 202760 | tf_op jit(solution)/shard_map/ppermute | solution.py:273
  26.0 6.6 %collective-permute-start.13 = (bf16[264,128]{1,0:T(8,128)(2,1)S(1)}, bf16[264,128]{1,0:T(8,128)(2,1)S(1)}, u32[]{:S(2)}, u32[]{:S(2)}) collective-permute-start(bf16[264,128]{1,0:T(8,128)(2,1)S(1)} %get-tuple-element.40), channel_id=1, source_target_pairs={{0,4},{4,0},{8,12},{12,8},{1,5},{5,1},{9,13},{13,9},{2,6},{6,2},{1... | collective-permute-start | bytes 202760 | tf_op jit(solution)/shard_map/ppermute | solution.py:273
  28.2 6.1 %collective-permute-start.10 = (bf16[264,128]{1,0:T(8,128)(2,1)S(1)}, bf16[264,128]{1,0:T(8,128)(2,1)S(1)}, u32[]{:S(2)}, u32[]{:S(2)}) collective-permute-start(bf16[264,128]{1,0:T(8,128)(2,1)S(1)} %get-tuple-element.37), channel_id=1, source_target_pairs={{0,12},{4,8},{8,4},{12,0},{1,13},{5,9},{9,5},{13,1},{2,14},{6,10},... | collective-permute-start | bytes 202760 | tf_op jit(solution)/shard_map/ppermute | solution.py:273
  28.7 7.3 %collective-permute-start.14 = (bf16[264,128]{1,0:T(8,128)(2,1)S(1)}, bf16[264,128]{1,0:T(8,128)(2,1)S(1)}, u32[]{:S(2)}, u32[]{:S(2)}) collective-permute-start(bf16[264,128]{1,0:T(8,128)(2,1)S(1)} %get-tuple-element.38.refs_0_), channel_id=1, source_target_pairs={{0,2},{2,0},{1,3},{3,1},{4,6},{6,4},{5,7},{7,5},{8,10},{10,8},{9,1... | collective-permute-start | bytes 202760 | tf_op jit(solution)/shard_map/ppermute | solution.py:262
  31.3 4.9 %collective-permute-start.15 = (bf16[264,128]{1,0:T(8,128)(2,1)S(1)}, bf16[264,128]{1,0:T(8,128)(2,1)S(1)}, u32[]{:S(2)}, u32[]{:S(2)}) collective-permute-start(bf16[264,128]{1,0:T(8,128)(2,1)S(1)} %collective-permute-done.12.refs_1_), channel_id=1, source_target_pairs={{0,2},{2,0},{1,3},{3,1},{4,6},{6,4},{5,7},{7,5},{8,10},{10,8},{9,1... | collective-permute-start | bytes 202760 | tf_op jit(solution)/shard_map/ppermute | solution.py:262
  32.6 4.8 %collective-permute-start.16 = (bf16[264,128]{1,0:T(8,128)(2,1)S(1)}, bf16[264,128]{1,0:T(8,128)(2,1)S(1)}, u32[]{:S(2)}, u32[]{:S(2)}) collective-permute-start(bf16[264,128]{1,0:T(8,128)(2,1)S(1)} %collective-permute-done.13.refs_2_), channel_id=1, source_target_pairs={{0,2},{2,0},{1,3},{3,1},{4,6},{6,4},{5,7},{7,5},{8,10},{10,8},{9,1... | collective-permute-start | bytes 202760 | tf_op jit(solution)/shard_map/ppermute | solution.py:262
  34.2 4.3 %collective-permute-start.11 = (bf16[264,128]{1,0:T(8,128)(2,1)S(1)}, bf16[264,128]{1,0:T(8,128)(2,1)S(1)}, u32[]{:S(2)}, u32[]{:S(2)}) collective-permute-start(bf16[264,128]{1,0:T(8,128)(2,1)S(1)} %collective-permute-done.10.refs_3_), channel_id=1, source_target_pairs={{0,2},{2,0},{1,3},{3,1},{4,6},{6,4},{5,7},{7,5},{8,10},{10,8},{9,1... | collective-permute-start | bytes 202760 | tf_op jit(solution)/shard_map/ppermute | solution.py:262
